TPU v7x, 512 devices: a whole 4x4x16 slice. The times are simulated.
512 devices in a mesh: dx: 16 (over x, y_lo, core), dy: 32 (over z, y_hi).
Axes of the slice: x: 4, y: 4 (y_hi: 2, y_lo: 2; y = y_hi * 2 + y_lo), z: 16, core: 2. Of those that a mesh axis runs over, the one named last changes fastest.
Arguments:
- image_emb: bfloat16 [131072, 1152], P(('dx', 'dy')), may hold values from -0.19921875 to 0.19921875
- text_feat: bfloat16 [131072, 1152], P(('dx', 'dy')), may hold values from -0.75 to 0.75
- text_head: bfloat16 [1152, 1152], replicated, may hold values from -0.1875 to 0.1875
- log_scale: float32 [1], replicated, may hold values from 1.6 to 2.3
- bias: float32 [1], replicated, may hold values from -3 to -1
Outputs:
- grad_image: float32 [131072, 1152], P(('dx', 'dy'))
- grad_text_feat: float32 [131072, 1152], P(('dx', 'dy'))
- grad_head: float32 [1152, 1152], P('dy', 'dx')
All inputs are finite; a program needn't handle non-finite values.
Results may differ from a plain program's by a relative error of at most 0.02.
Values may be sent and summed in bfloat16 or wider, within the bound.
No kernel may reach another device: no remote copies, remote signals or barrier semaphores. Data moves between devices by JAX's collectives and lax.ppermute only.
A program may use at most 64 MiB of HBM per device.

v0:
```python
import jax
import jax.numpy as jnp
from jax import lax
from jax.sharding import PartitionSpec as P

STEPS = 4


def from_behind(value, axis, steps):
    count = lax.axis_size(axis)
    pairs = [(source, (source + steps) % count) for source in range(count)]
    return lax.ppermute(value, axis, pairs)


def unit_rows(values):
    row_norm = jnp.sqrt(jnp.sum(values * values, axis=-1, keepdims=True) + 1e-06)
    return (values / row_norm, row_norm)


def pair_weight(image_low, text_low, sign_values, temper, offset):
    products = lax.dot_general(
        image_low, text_low, (((1,), (1,)), ((), ())), preferred_element_type=jnp.float32
    )
    logits = temper * products + offset
    return (-sign_values * jax.nn.sigmoid(-sign_values * logits) * temper).astype(jnp.bfloat16)


def pair_grads(image_low, text_low, sign_values, temper, offset):
    weight = pair_weight(image_low, text_low, sign_values, temper, offset)
    image_part = jnp.dot(weight, text_low, preferred_element_type=jnp.float32)
    text_part = lax.dot_general(
        weight, image_low, (((0,), (0,)), ((), ())), preferred_element_type=jnp.float32
    )
    return (image_part, text_part)


def local(image_emb, text_feat, text_head, log_scale, bias):
    temper = jnp.exp(log_scale[0])
    offset = bias[0]
    image_unit, image_norm = unit_rows(image_emb.astype(jnp.float32))
    image_low = image_unit.astype(jnp.bfloat16)
    text_raw = jnp.dot(text_feat, text_head, preferred_element_type=jnp.float32)
    text_unit, text_norm = unit_rows(text_raw)
    text_low = text_unit.astype(jnp.bfloat16)
    row_count = image_low.shape[0]
    diagonal_mask = lax.broadcasted_iota(
        jnp.int32, (row_count, row_count), 0
    ) == lax.broadcasted_iota(jnp.int32, (row_count, row_count), 1)
    sign_diag = jnp.where(diagonal_mask, 1.0, -1.0).astype(jnp.float32)
    other_sign = jnp.float32(-1.0)
    image_sum, text_sum = pair_grads(image_low, text_low, sign_diag, temper, offset)
    visitor = text_low
    carried = text_sum
    for distance in range(1, STEPS):
        visitor = from_behind(visitor, "dy", 1)
        image_part, text_part = pair_grads(image_low, visitor, other_sign, temper, offset)
        image_sum = image_sum + image_part
        if distance == 1:
            carried = text_part
        else:
            carried = from_behind(carried, "dy", 1) + text_part
    text_sum = text_sum + from_behind(carried, "dy", 1 - STEPS)
    along = jnp.sum(image_unit * image_sum, axis=-1, keepdims=True)
    grad_image = (image_sum - image_unit * along) / image_norm
    along_text = jnp.sum(text_unit * text_sum, axis=-1, keepdims=True)
    text_back = ((text_sum - text_unit * along_text) / text_norm).astype(jnp.bfloat16)
    grad_feat = lax.dot_general(
        text_back, text_head, (((1,), (1,)), ((), ())), preferred_element_type=jnp.float32
    )
    outer_part = lax.psum_scatter(
        lax.dot_general(
            text_back, text_feat, (((0,), (0,)), ((), ())), preferred_element_type=jnp.float32
        ).astype(jnp.bfloat16),
        "dx",
        scatter_dimension=0,
        tiled=True,
    ).astype(jnp.float32)
    grad_head = lax.psum_scatter(outer_part, "dy", scatter_dimension=1, tiled=True).T
    return (grad_image, grad_feat, grad_head)


def solution(mesh):
    return jax.shard_map(
        local,
        mesh=mesh,
        in_specs=(P(("dx", "dy"), None), P(("dx", "dy"), None), P(), P(), P()),
        out_specs=(P(("dx", "dy"), None), P(("dx", "dy"), None), P("dy", "dx")),
        check_vma=False,
    )
```

profile of v0, /device:TPU:24, one launch (start us, length us, event | category | flops | bytes accessed | tf_op | source)
XLA Modules:
  0.0 408.0 jit_solution(1734167527906927369)
XLA Ops:
  7.2 0.0 copy-start
  7.2 0.0 reduce-scatter.6.cloned.1.call-start
  7.2 1.7 copy-done
  8.9 2.1 multiply_reduce_fusion.2
  11.1 0.1 fusion.32
  11.3 4.5 %collective-permute-start = (bf16[256,1152]{1,0:T(8,128)(2,1)S(1)}, bf16[256,1152]{1,0:T(8,128)(2,1)S(1)}, u32[]{:S(2)}, u32[]{:S(2)}) collective-permute-start(bf16[256,1152]{1,0:T(8,128)(2,1)S(1)} %fusion.32), channel_id=1, source_target_pairs={{0,1},{1,2},{2,3},{3,4},{4,5},{5,6},{6,7},{7,8},{8,9},{9,10},{10,1... | collective-permute-start | bytes 1769480 | tf_op jit(solution)/shard_map/ppermute | solution.py:12
  15.8 0.2 fusion
  17.3 0.2 fusion.31
  17.5 12.2 %collective-permute-done = bf16[256,1152]{1,0:T(8,128)(2,1)S(1)} collective-permute-done((bf16[256,1152]{1,0:T(8,128)(2,1)S(1)}, bf16[256,1152]{1,0:T(8,128)(2,1)S(1)}, u32[]{:S(2)}, u32[]{:S(2)}) %collective-permute-start) | collective-permute-done | bytes 589856 | tf_op jit(solution)/shard_map/ppermute | solution.py:12
  29.7 0.4 fusion.28
  30.1 0.4 fusion.35
  30.5 5.4 %collective-permute-start.3 = (f32[256,1152]{1,0:T(8,128)S(1)}, f32[256,1152]{1,0:T(8,128)S(1)}, u32[]{:S(2)}, u32[]{:S(2)}) collective-permute-start(f32[256,1152]{1,0:T(8,128)S(1)} %fusion.35), channel_id=1, source_target_pairs={{0,1},{1,2},{2,3},{3,4},{4,5},{5,6},{6,7},{7,8},{8,9},{9,10},{10,1... | collective-permute-start | bytes 3538952 | tf_op jit(solution)/shard_map/ppermute | solution.py:12
  35.9 3.3 collective-permute-start.1
  39.2 40.4 %collective-permute-done.1 = bf16[256,1152]{1,0:T(8,128)(2,1)S(1)} collective-permute-done((bf16[256,1152]{1,0:T(8,128)(2,1)S(1)}, bf16[256,1152]{1,0:T(8,128)(2,1)S(1)}, u32[]{:S(2)}, u32[]{:S(2)}) %collective-permute-start.1) | collective-permute-done | bytes 589856 | tf_op jit(solution)/shard_map/ppermute | solution.py:12
  79.7 0.4 fusion.29
  80.1 0.4 convolution_add_fusion
  80.5 1.9 collective-permute-start.4
  82.4 1.9 collective-permute-start.2
  84.3 40.5 %collective-permute-done.2 = bf16[256,1152]{1,0:T(8,128)(2,1)S(1)} collective-permute-done((bf16[256,1152]{1,0:T(8,128)(2,1)S(1)}, bf16[256,1152]{1,0:T(8,128)(2,1)S(1)}, u32[]{:S(2)}, u32[]{:S(2)}) %collective-permute-start.2) | collective-permute-done | bytes 589856 | tf_op jit(solution)/shard_map/ppermute | solution.py:12
  124.9 0.4 fusion.30
  125.3 0.4 copy-done.13
  125.7 0.4 fusion.36
  126.1 0.2 add.83
  126.2 0.1 copy-done.11
  126.3 6.0 %collective-permute-start.5 = (f32[256,1152]{1,0:T(8,128)S(1)}, f32[256,1152]{1,0:T(8,128)S(1)}, u32[]{:S(2)}, u32[]{:S(2)}) collective-permute-start(f32[256,1152]{1,0:T(8,128)S(1)} %add.83), channel_id=1, source_target_pairs={{0,29},{1,30},{2,31},{3,0},{4,1},{5,2},{6,3},{7,4},{8,5},{9,6},{10... | collective-permute-start | bytes 3538952 | tf_op jit(solution)/shard_map/ppermute | solution.py:12
  132.4 0.4 fusion.27
  132.8 0.4 fusion.34
  133.2 0.3 copy-done.10
  133.5 42.7 %collective-permute-done.5 = f32[256,1152]{1,0:T(8,128)S(1)} collective-permute-done((f32[256,1152]{1,0:T(8,128)S(1)}, f32[256,1152]{1,0:T(8,128)S(1)}, u32[]{:S(2)}, u32[]{:S(2)}) %collective-permute-start.5) | collective-permute-done | bytes 1179680 | tf_op jit(solution)/shard_map/ppermute | solution.py:12
  176.2 0.3 multiply_reduce_fusion
  176.5 0.3 divide_convert_fusion
  176.7 0.8 copy-done.2
  177.5 2.5 convolution_convert_fusion
  180.1 0.0 reduce-scatter.6.cloned.1.call-update
  180.1 1.3 dynamic-slice.2
  182.0 1.5 fusion.33
  183.6 0.3 convolution_add_fusion.3
  183.9 0.7 copy-done.9
  184.6 0.3 convolution_add_fusion.2
  185.0 0.6 copy-done.12
  185.5 0.2 copy-done.14
  185.8 0.4 multiply_reduce_fusion.1
  186.2 1.3 subtract_divide_fusion
  187.5 2.1 fusion.37
  189.6 63.7 %reduce-scatter.6.cloned.1.call-done = bf16[72,1152]{1,0:T(8,128)(2,1)} async-done(((bf16[1152,1152]{1,0:T(8,128)(2,1)}), bf16[72,1152]{1,0:T(8,128)(2,1)}) %reduce-scatter.6.cloned.1.call-update) | async-done | bytes 165904
  253.3 147.1 %all-reduce.3 = f32[72,1152]{1,0:T(8,128)S(1)} all-reduce(bf16[72,1152]{1,0:T(8,128)(2,1)} %reduce-scatter.6.cloned.1.call-done), channel_id=3, replica_groups=mesh['dx'=16,'dy'=32] {'dy'}, use_global_device_ids=true, to_apply=%region_5.6.clone | all-reduce | flops 82944 | bytes 497664
  400.4 0.1 dynamic-slice_bitcast_fusion
  400.5 0.7 copy.9
  (25 shorter events, 0.1 us)
Async XLA Ops:
  7.2 1.8 copy-start
  7.2 246.2 %reduce-scatter.6.cloned.1.call-start = ((), (), s32[]{:S(2)}) async-start(), calls=%async_computation.1 | async-start | bytes 2820096
  11.1 4.7 %copy-start.1 = (bf16[256,1152]{1,0:T(8,128)(2,1)S(1)}, bf16[256,1152]{1,0:T(8,128)(2,1)}, u32[]{:S(2)}) copy-start(bf16[256,1152]{1,0:T(8,128)(2,1)} %param.5) | copy-start | bytes 1769476
  11.2 121.1 %copy-start.4 = (bf16[256,1152]{1,0:T(8,128)(2,1)}, bf16[256,1152]{1,0:T(8,128)(2,1)S(1)}, u32[]{:S(2)}) copy-start(bf16[256,1152]{1,0:T(8,128)(2,1)S(1)} %fusion.32) | copy-start | bytes 1769476
  11.3 18.5 %collective-permute-start = (bf16[256,1152]{1,0:T(8,128)(2,1)S(1)}, bf16[256,1152]{1,0:T(8,128)(2,1)S(1)}, u32[]{:S(2)}, u32[]{:S(2)}) collective-permute-start(bf16[256,1152]{1,0:T(8,128)(2,1)S(1)} %fusion.32), channel_id=1, source_target_pairs={{0,1},{1,2},{2,3},{3,4},{4,5},{5,6},{6,7},{7,8},{8,9},{9,10},{10,1... | collective-permute-start | bytes 1769480 | tf_op jit(solution)/shard_map/ppermute | solution.py:12
  29.7 6.2 %copy-start.6 = (bf16[256,1152]{1,0:T(8,128)(2,1)}, bf16[256,1152]{1,0:T(8,128)(2,1)S(1)}, u32[]{:S(2)}) copy-start(bf16[256,1152]{1,0:T(8,128)(2,1)S(1)} %collective-permute-done) | copy-start | bytes 1769476
  30.5 49.6 %collective-permute-start.3 = (f32[256,1152]{1,0:T(8,128)S(1)}, f32[256,1152]{1,0:T(8,128)S(1)}, u32[]{:S(2)}, u32[]{:S(2)}) collective-permute-start(f32[256,1152]{1,0:T(8,128)S(1)} %fusion.35), channel_id=1, source_target_pairs={{0,1},{1,2},{2,3},{3,4},{4,5},{5,6},{6,7},{7,8},{8,9},{9,10},{10,1... | collective-permute-start | bytes 3538952 | tf_op jit(solution)/shard_map/ppermute | solution.py:12
  35.9 43.8 %collective-permute-start.1 = (bf16[256,1152]{1,0:T(8,128)(2,1)S(1)}, bf16[256,1152]{1,0:T(8,128)(2,1)S(1)}, u32[]{:S(2)}, u32[]{:S(2)}) collective-permute-start(bf16[256,1152]{1,0:T(8,128)(2,1)S(1)} %collective-permute-done), channel_id=1, source_target_pairs={{0,1},{1,2},{2,3},{3,4},{4,5},{5,6},{6,7},{7,8},{8,9},{9,10},{10,1... | collective-permute-start | bytes 1769480 | tf_op jit(solution)/shard_map/ppermute | solution.py:12
  79.7 2.7 copy-start.8
  80.5 45.6 %collective-permute-start.4 = (f32[256,1152]{1,0:T(8,128)S(1)}, f32[256,1152]{1,0:T(8,128)S(1)}, u32[]{:S(2)}, u32[]{:S(2)}) collective-permute-start(f32[256,1152]{1,0:T(8,128)S(1)} %convolution_add_fusion), channel_id=1, source_target_pairs={{0,1},{1,2},{2,3},{3,4},{4,5},{5,6},{6,7},{7,8},{8,9},{9,10},{10,1... | collective-permute-start | bytes 3538952 | tf_op jit(solution)/shard_map/ppermute | solution.py:12
  82.4 42.4 %collective-permute-start.2 = (bf16[256,1152]{1,0:T(8,128)(2,1)S(1)}, bf16[256,1152]{1,0:T(8,128)(2,1)S(1)}, u32[]{:S(2)}, u32[]{:S(2)}) collective-permute-start(bf16[256,1152]{1,0:T(8,128)(2,1)S(1)} %collective-permute-done.1), channel_id=1, source_target_pairs={{0,1},{1,2},{2,3},{3,4},{4,5},{5,6},{6,7},{7,8},{8,9},{9,10},{10,1... | collective-permute-start | bytes 1769480 | tf_op jit(solution)/shard_map/ppermute | solution.py:12
  124.9 0.8 copy-start.13
  125.7 0.7 copy-start.11
  126.3 49.8 %collective-permute-start.5 = (f32[256,1152]{1,0:T(8,128)S(1)}, f32[256,1152]{1,0:T(8,128)S(1)}, u32[]{:S(2)}, u32[]{:S(2)}) collective-permute-start(f32[256,1152]{1,0:T(8,128)S(1)} %add.83), channel_id=1, source_target_pairs={{0,29},{1,30},{2,31},{3,0},{4,1},{5,2},{6,3},{7,4},{8,5},{9,6},{10... | collective-permute-start | bytes 3538952 | tf_op jit(solution)/shard_map/ppermute | solution.py:12
  132.8 0.7 copy-start.10
  176.5 1.1 copy-start.5
  176.7 0.8 copy-start.2
  182.0 1.5 copy-start.7
  183.6 1.1 copy-start.9
  184.6 0.9 copy-start.12
  184.6 1.1 copy-start.14
  186.2 1.3 copy-start.3
Sparse Core Ops, SparseCore 0:
  180.2 73.0 reduce-scatter.5
where the time goes:
time: 416 us; the launch traced here: 408 us
  waiting for transfers between devices  200 us (48%)
  blocking collectives  147 us (35%)
  starting transfers between devices  23.1 us (6%)
  between operations  16.3 us (4%)
  matrix products  12.5 us (3%)
  local copies, waits for them, and re-layouts  6.9 us (2%)
    unnamed x1, blocking collectives  147 us
    ppermute x6, waiting for transfers between devices, from_behind(): return lax.ppermute(value, axis, pairs)  136 us
    unnamed x2, waiting for transfers between devices  63.8 us
    ppermute x6, starting transfers between devices, from_behind(): return lax.ppermute(value, axis, pairs)  23.1 us
  transfers between devices with their start and end apart: 7, of which 5 were waited for; matrix products, arithmetic and copies ran while one was open for 2% of the time, Pallas kernels for 0%

commit v1 on v0

v1 whole, which is shorter than its diff:
```python
import jax
import jax.numpy as jnp
import numpy as np
from jax import lax
from jax.experimental import pallas as pl
from jax.experimental.pallas import tpu as pltpu
from jax.sharding import PartitionSpec as P

NX, NYL, NC, NZ, NYH = 4, 2, 2, 16, 2
N_DX, N_DY = NX * NYL * NC, NZ * NYH
LANES = 128
VMEM = pl.BlockSpec(memory_space=pltpu.VMEM)
SMEM = pl.BlockSpec(memory_space=pltpu.SMEM)
LIMIT = pltpu.CompilerParams(vmem_limit_bytes=12 << 20)


def unit_rows(values):
    row_norm = jnp.sqrt(jnp.sum(values * values, axis=-1, keepdims=True) + 1e-06)
    return (values / row_norm, row_norm)


def shifted(value, x_steps, dy_steps):
    if x_steps == 0:
        pairs = [(s, (s + dy_steps) % N_DY) for s in range(N_DY)]
        return lax.ppermute(value, "dy", pairs)
    step = NYL * NC
    if dy_steps == 0:
        return lax.ppermute(value, "dx", [(s, (s + step * x_steps) % N_DX) for s in range(N_DX)])
    pairs = [
        (p * N_DY + q, (p + step * x_steps) % N_DX * N_DY + (q + dy_steps) % N_DY)
        for p in range(N_DX)
        for q in range(N_DY)
    ]
    return lax.ppermute(value, ("dx", "dy"), pairs)


def dot_nt(left, right):
    return lax.dot_general(left, right, (((1,), (1,)), ((), ())), preferred_element_type=jnp.float32)


def dot_tn(left, right):
    return lax.dot_general(left, right, (((0,), (0,)), ((), ())), preferred_element_type=jnp.float32)


def dot_nn(left, right):
    return jnp.dot(left, right, preferred_element_type=jnp.float32)


def unit_scaled(values):
    scale = 1.0 / jnp.sqrt(jnp.sum(values * values, axis=-1, keepdims=True) + 1e-06)
    return (values * scale, scale)


def weight_turned(text_low, image_low, sign_values, temper, offset):
    logits = temper * dot_nt(text_low, image_low) + offset
    return (-sign_values * jax.nn.sigmoid(-sign_values * logits) * temper).astype(jnp.bfloat16)


def back_of(text_sum, text_unit, scale):
    along = jnp.sum(text_unit * text_sum, axis=-1, keepdims=True)
    return (text_sum - text_unit * along) * scale


def own_kernel(
    scale_ref,
    feat_ref,
    head_ref,
    image_ref,
    target_ref,
    spread_ref,
    sorted_ref,
    unit_ref,
    scale_col_ref,
    text_low_ref,
    image_low_ref,
    weight_ref,
    first_ref,
):
    rows = feat_ref.shape[0]
    text_unit, scale = unit_scaled(dot_nn(feat_ref[...], head_ref[...]))
    unit_ref[...] = text_unit
    scale_col_ref[...] = scale
    text_low = text_unit.astype(jnp.bfloat16)
    text_low_ref[...] = text_low
    image_low = unit_scaled(image_ref[...].astype(jnp.float32))[0].astype(jnp.bfloat16)
    image_low_ref[...] = image_low
    grid = [lax.broadcasted_iota(jnp.int32, (rows, rows), axis) for axis in range(2)]
    sign_diag = jnp.where(grid[0] == grid[1], 1.0, -1.0)
    weight = weight_turned(text_low, image_low, sign_diag, scale_ref[0], scale_ref[1])
    weight_ref[...] = weight
    first_ref[...] = dot_nn(weight, image_low)
    lane = lax.broadcasted_iota(jnp.int32, spread_ref.shape, 1)
    spread = jnp.where(lane == target_ref[...], 1.0, 0.0).astype(jnp.bfloat16)
    spread_ref[...] = spread
    sorted_ref[...] = dot_nn(feat_ref[...], spread).astype(jnp.bfloat16)


def arrive_kernel(
    core_ref,
    scale_ref,
    visit_ref,
    image_ref,
    head_ref,
    spread_ref,
    image_low_ref,
    text_low_ref,
    unit_ref,
    scale_col_ref,
    first_ref,
    image_far_ref,
    text_next_ref,
    weight_far_ref,
    weight_on_ref,
    weight_fn_ref,
    own_ref,
    part_ref,
    sorted_ref,
    mine_ref,
    other_ref,
    turned_ref,
):
    temper, offset = scale_ref[0], scale_ref[1]
    rows = visit_ref.shape[0]
    image_far = unit_scaled(image_ref[...].astype(jnp.float32))[0].astype(jnp.bfloat16)
    image_far_ref[...] = image_far
    weight_far = weight_turned(text_low_ref[...], image_far, -1.0, temper, offset)
    weight_far_ref[...] = weight_far
    text_own = first_ref[...] + dot_nn(weight_far, image_far)
    own_ref[...] = text_own
    turned_ref[:, :rows] = back_of(text_own, unit_ref[...], scale_col_ref[...]).T

    next_unit, next_scale = unit_scaled(dot_nn(visit_ref[...], head_ref[...]))
    text_next = next_unit.astype(jnp.bfloat16)
    text_next_ref[...] = text_next
    weight_on = weight_turned(text_next, image_low_ref[...], -1.0, temper, offset)
    weight_on_ref[...] = weight_on
    weight_fn = weight_turned(text_next, image_far, -1.0, temper, offset)
    weight_fn_ref[...] = weight_fn
    text_part = dot_nn(weight_on, image_low_ref[...]) + dot_nn(weight_fn, image_far)
    part_ref[...] = text_part.astype(jnp.bfloat16)
    turned_ref[:, rows:] = back_of(text_part, next_unit, next_scale).T
    sorted_ref[...] = dot_nn(visit_ref[...], spread_ref[...]).astype(jnp.bfloat16)

    pieces = NX * NYL
    share = turned_ref.shape[0] // (pieces * NC)
    for out_ref, core in ((mine_ref, core_ref[0]), (other_ref, 1 - core_ref[0])):
        starts = [pl.multiple_of((g * NC + core) * share, 8) for g in range(pieces)]
        cols = [turned_ref[pl.ds(start, share), :] for start in starts]
        out_ref[...] = jnp.concatenate(cols, axis=0).astype(jnp.bfloat16)


def in_vmem(kernel, scalars, arrays, shapes, macs, name, scratch=()):
    return pl.pallas_call(
        kernel,
        in_specs=[SMEM] * len(scalars) + [VMEM] * len(arrays),
        out_specs=[VMEM] * len(shapes),
        out_shape=[jax.ShapeDtypeStruct(*shape) for shape in shapes],
        scratch_shapes=scratch,
        compiler_params=pltpu.CompilerParams(vmem_limit_bytes=12 << 20),
        cost_estimate=pl.CostEstimate(flops=2 * macs, bytes_accessed=8 << 20, transcendentals=0),
        name=name,
    )(*scalars, *arrays)


def in_tiles(block):
    rows, cols = block.shape
    whole, left = cols // LANES, cols % LANES
    high = tail_rows(rows)
    tail = block[:, whole * LANES :]
    blank = jnp.zeros((2 * high - rows, left), block.dtype)
    tail = jnp.concatenate([tail[:high], jnp.concatenate([tail[high:], blank], axis=0)], axis=1)
    tiles = [block[:, t * LANES : (t + 1) * LANES] for t in range(whole)]
    return jnp.concatenate(tiles + [tail], axis=0)


def from_tiles(tiles, rows, cols):
    whole, left = cols // LANES, cols % LANES
    high = tail_rows(rows)
    tail = tiles[whole * rows :]
    tail = jnp.concatenate([tail[:, :left], tail[: rows - high, left : 2 * left]], axis=0)
    parts = [tiles[t * rows : (t + 1) * rows] for t in range(whole)]
    return jnp.concatenate(parts + [tail], axis=1)


def tail_rows(rows):
    return -(-rows // 2 // 8) * 8


def product_kernel(back_ref, feat_ref, visit_ref, *rest):
    out_ref = rest[-1]
    rows = feat_ref.shape[0]
    share = back_ref.shape[0] // (NX * NYL)
    used = back_ref.shape[0] * NC // NYH
    half = feat_ref.shape[1] // NYH
    lanes = pl.ds(pl.multiple_of(pl.program_id(0) * half, LANES), half)
    total = dot_nn(back_ref[:, :rows], feat_ref[:, lanes])
    total += dot_nn(back_ref[:, rows:], visit_ref[:, lanes])
    for part in range(NX * NYL):
        cut = in_tiles(total[part * share : (part + 1) * share, :used])
        if len(rest) > 1:
            cut += rest[0][part, pl.program_id(0)].astype(jnp.float32)
        out_ref[part, 0] = cut.astype(jnp.bfloat16)


def head_product(back, feat, visit, *added):
    cols, rows = back.shape
    width = feat.shape[1]
    parts = NX * NYL
    share, used = cols // parts, cols * NC // NYH
    high = used // LANES * share + tail_rows(share)
    return pl.pallas_call(
        product_kernel,
        grid=(NYH,),
        in_specs=[VMEM] * (3 + len(added)),
        out_specs=pl.BlockSpec((parts, 1, high, LANES), lambda i: (0, i, 0, 0)),
        out_shape=jax.ShapeDtypeStruct((parts, NYH, high, LANES), jnp.bfloat16),
        compiler_params=LIMIT,
        cost_estimate=pl.CostEstimate(flops=2 * cols * rows * width, bytes_accessed=4 << 20, transcendentals=0),
        name="head_product",
    )(back, feat, visit, *added)


def pack_kernel(parts_ref, out_ref):
    slots, high, _ = out_ref.shape
    share, used = 3 * high, 3 * high * N_DX // NYH
    total = from_tiles(jnp.sum(parts_ref[...].astype(jnp.float32), axis=0), share, used)
    wide = total.shape[1] // slots
    blank = jnp.zeros((high, LANES - total.shape[0] // high * wide), jnp.float32)
    for z in range(slots):
        piece = total[:, z * wide : (z + 1) * wide]
        pieces = [piece[g * high : (g + 1) * high] for g in range(total.shape[0] // high)]
        out_ref[z] = jnp.concatenate(pieces + [blank], axis=1).astype(jnp.bfloat16)


def summed_and_packed(parts, share):
    return pl.pallas_call(
        pack_kernel,
        in_specs=[VMEM],
        out_specs=VMEM,
        out_shape=jax.ShapeDtypeStruct((NZ, share // 3, LANES), jnp.bfloat16),
        compiler_params=LIMIT,
        name="sum_x_y",
    )(parts)


def unpack_kernel(parts_ref, out_ref):
    total = jnp.sum(parts_ref[...].astype(jnp.float32), axis=0)
    wide, share = out_ref.shape
    high = total.shape[0]
    pieces = [total[:, g * wide : (g + 1) * wide] for g in range(share // high)]
    piece = jnp.concatenate(pieces, axis=0)
    piece = jnp.concatenate([piece, jnp.zeros((share, LANES - wide), jnp.float32)], axis=1)
    piece = jnp.concatenate([piece, jnp.zeros((LANES - share, LANES), jnp.float32)], axis=0)
    out_ref[...] = piece.T[:wide, :share]


def summed_over_z(parts, wide, share):
    return pl.pallas_call(
        unpack_kernel,
        in_specs=[VMEM],
        out_specs=VMEM,
        out_shape=jax.ShapeDtypeStruct((wide, share), jnp.float32),
        compiler_params=LIMIT,
        name="sum_z",
    )(parts)


def text_back_kernel(own_ref, home_ref, unit_ref, scale_col_ref, out_ref):
    text_sum = own_ref[...] + home_ref[...].astype(jnp.float32)
    out_ref[...] = back_of(text_sum, unit_ref[...], scale_col_ref[...]).astype(jnp.bfloat16)


def grad_image_kernel(own_ref, home_ref, image_ref, out_ref):
    image_sum = own_ref[...] + home_ref[...].astype(jnp.float32)
    image_unit, scale = unit_scaled(image_ref[...].astype(jnp.float32))
    out_ref[...] = back_of(image_sum, image_unit, scale)


def by_rows(kernel, arrays, dtype, flops, name):
    rows, width = arrays[0].shape
    tile = rows // 2
    return pl.pallas_call(
        kernel,
        grid=(rows // tile,),
        in_specs=[pl.BlockSpec((tile, array.shape[1]), lambda i: (i, 0)) for array in arrays],
        out_specs=pl.BlockSpec((tile, width), lambda i: (i, 0)),
        out_shape=jax.ShapeDtypeStruct((rows, width), dtype),
        compiler_params=LIMIT,
        cost_estimate=pl.CostEstimate(flops=flops, bytes_accessed=4 << 20, transcendentals=0),
        name=name,
    )(*arrays)


def local(image_emb, text_feat, text_head, log_scale, bias):
    rows, width = image_emb.shape
    wide = width // N_DY
    share = width // N_DX
    temper = jnp.exp(log_scale[0])
    offset = bias[0]
    scales = jnp.stack([temper, offset])
    core = (lax.axis_index("dx") % NC).astype(jnp.int32).reshape(1)

    low, high = jnp.bfloat16, jnp.float32

    text_visit = shifted(text_feat, 0, 1)
    image_visit = shifted(image_emb, 0, -2)

    half = -(-width // NYH // LANES) * LANES
    place = np.arange(width)
    target = place // wide % NYH * half + place // (wide * NYH) * wide + place % wide
    target = jnp.asarray(target.reshape(width, 1), jnp.int32)
    block, square, column = (rows, width), (rows, rows), (rows, 1)
    sort = (rows, NYH * half)
    own = in_vmem(
        own_kernel,
        [scales],
        [text_feat, text_head, image_emb, target],
        [((width, NYH * half), low), (sort, low), (block, high), (column, high)]
        + [(block, low), (block, low), (square, low), (block, high)],
        rows * width * (width + 2 * rows + NYH * half),
        "own_blocks",
    )
    spread, feat_sorted, text_unit, text_scale, text_low, image_low, weight_own, text_first = own
    out = in_vmem(
        arrive_kernel,
        [core, scales],
        [text_visit, image_visit, text_head, spread, image_low, text_low, text_unit, text_scale, text_first],
        [(block, low), (block, low), (square, low), (square, low), (square, low), (block, high)]
        + [(block, low), (sort, low)]
        + [((width // NC, 2 * rows), low)] * 2,
        rows * width * (width + 6 * rows + NYH * half),
        "arrived",
        [pltpu.VMEM((width, 2 * rows), jnp.float32)],
    )
    image_far, text_next, weight_far, weight_on, weight_fn, text_own, text_part = out[:7]
    visit_sorted, back_mine, back_other = out[7:]

    head_other = head_product(back_other, feat_sorted, visit_sorted)
    head_in = lax.ppermute(head_other, "dx", [(p, p ^ 1) for p in range(N_DX)])
    text_part, _ = lax.optimization_barrier((text_part, head_other))
    text_home = shifted(text_part, 0, -1)
    head_part = head_product(back_mine, feat_sorted, visit_sorted, head_in)
    head_part = head_part.reshape(-1, *head_part.shape[2:])
    groups = [
        [
            ((x * NYL + yl) * NC + c) * N_DY + z * NYH + yh
            for x in range(NX)
            for yl in range(NYL)
            for yh in range(NYH)
        ]
        for c in range(NC)
        for z in range(NZ)
    ]
    late = (weight_own, weight_far, weight_on, weight_fn, text_own, head_part)
    weight_own, weight_far, weight_on, weight_fn, text_own, _ = lax.optimization_barrier(late)
    head_part = lax.all_to_all(head_part, ("dx", "dy"), 0, 0, axis_index_groups=groups, tiled=True)
    head_part = summed_and_packed(head_part, share)

    text_back = by_rows(
        text_back_kernel, [text_own, text_home, text_unit, text_scale], low, 2 * 10**10, "text_back"
    )
    image_part = dot_tn(weight_far, text_low) + dot_tn(weight_fn, text_next)
    image_home = shifted(image_part.astype(jnp.bfloat16), 0, 2)
    image_own = dot_tn(weight_own, text_low) + dot_tn(weight_on, text_next)

    late = (image_own, text_back, image_emb, head_part)
    image_own, text_back, image_emb, head_part = lax.optimization_barrier(late)
    groups = [[z * NYH + yh for z in range(NZ)] for yh in range(NYH)]
    head_part = lax.all_to_all(head_part, "dy", 0, 0, axis_index_groups=groups, tiled=True)
    grad_head = summed_over_z(head_part, wide, share)
    grad_image = by_rows(
        grad_image_kernel, [image_own, image_home, image_emb], high, 8 * rows * width, "grad_image"
    )
    grad_feat = dot_nt(text_back, text_head)
    return (grad_image, grad_feat, grad_head)


def solution(mesh):
    return jax.shard_map(
        local,
        mesh=mesh,
        in_specs=(P(("dx", "dy"), None), P(("dx", "dy"), None), P(), P(), P()),
        out_specs=(P(("dx", "dy"), None), P(("dx", "dy"), None), P("dy", "dx")),
        check_vma=False,
    )
```

time: 416 us -> 99.7 us (0.24); the launches traced: 408 us -> 99.1 us
  waiting for transfers between devices: 200 us -> 27.8 us
  blocking collectives: 147 us -> 0 us
  Pallas kernels: 0 us -> 18.8 us
  starting transfers between devices: 23.1 us -> 40.4 us
  between operations: 16.3 us -> 2.2 us
  matrix products: 12.5 us -> 4.37 us
    unnamed x1 -> x0, blocking collectives: 147 us -> none
    ppermute x6 -> x5, waiting for transfers between devices: 136 us -> 4.06 us  [the longest x4 4.05 us: shifted(): return lax.ppermute(value, 'dy', pairs)]
    unnamed x2 -> x0, waiting for transfers between devices: 63.8 us -> none
    all_to_all x0 -> x2, waiting for transfers between devices: none -> 23.7 us  [the longest x1 15 us: local(): lax.all_to_all(head_part, ('dx', 'dy'), 0, 0, axis_index_groups=groups, t...]
    pallas_call x0 -> x8, Pallas kernels: none -> 18.8 us  [the longest x2 9.39 us: in_vmem(): pl.pallas_call(kernel, in_specs=[SMEM] * len(scalars) + [VMEM] * len(arra...]
    all_to_all x0 -> x2, starting transfers between devices: none -> 17.9 us  [the longest x1 10.2 us: local(): lax.all_to_all(head_part, 'dy', 0, 0, axis_index_groups=groups, tiled=True)]
    dot_general x15 -> x5, matrix products: 12.5 us -> 4.37 us  [the longest x4 2.3 us: dot_tn(): lax.dot_general(left, right, (((0,), (0,)), ((), ())), preferred_element_...]
    ppermute x6 -> x5, starting transfers between devices: 23.1 us -> 22.4 us  [the longest x4 20.5 us: shifted(): return lax.ppermute(value, 'dy', pairs)]
  transfers between devices with their start and end apart: 7 -> 7, of which waited for: 5 -> 4; matrix products, arithmetic and copies ran while one was open for 2% -> 4% of each run, Pallas kernels for 0% -> 11%
where the time goes in v1:
time: 99.7 us; the launch traced here: 99.1 us
  starting transfers between devices  40.4 us (41%)
  waiting for transfers between devices  27.8 us (28%)
  Pallas kernels  18.8 us (19%)
  local copies, waits for them, and re-layouts  5.44 us (5%)
  matrix products  4.37 us (4%)
  between operations  2.2 us (2%)
    ppermute x4, starting transfers between devices, shifted(): return lax.ppermute(value, 'dy', pairs)  20.5 us
    all_to_all x1, waiting for transfers between devices, local(): lax.all_to_all(head_part, ('dx', 'dy'), 0, 0, axis_index_groups=groups, t...  15 us
    all_to_all x1, starting transfers between devices, local(): lax.all_to_all(head_part, 'dy', 0, 0, axis_index_groups=groups, tiled=True)  10.2 us
    pallas_call x2, Pallas kernels, in_vmem(): pl.pallas_call(kernel, in_specs=[SMEM] * len(scalars) + [VMEM] * len(arra...  9.39 us
    all_to_all x1, waiting for transfers between devices, local(): lax.all_to_all(head_part, 'dy', 0, 0, axis_index_groups=groups, tiled=True)  8.67 us
    all_to_all x1, starting transfers between devices, local(): lax.all_to_all(head_part, ('dx', 'dy'), 0, 0, axis_index_groups=groups, t...  7.76 us
    unnamed x32, local copies, waits for them, and re-layouts  5.44 us
    ppermute x4, waiting for transfers between devices, shifted(): return lax.ppermute(value, 'dy', pairs)  4.05 us
  transfers between devices with their start and end apart: 7, of which 4 were waited for; matrix products, arithmetic and copies ran while one was open for 4% of the time, Pallas kernels for 11%

profile of v1, /device:TPU:24, one launch (start us, length us, event | category | flops | bytes accessed | tf_op | source)
XLA Modules:
  0.0 99.1 jit_solution(8731963625483665050)
XLA Ops:
  0.6 4.5 %collective-permute-start = (bf16[256,1152]{1,0:T(8,128)(2,1)}, bf16[256,1152]{1,0:T(8,128)(2,1)S(1)}, u32[]{:S(2)}, u32[]{:S(2)}) collective-permute-start(bf16[256,1152]{1,0:T(8,128)(2,1)} %feat_ref.1), channel_id=1, source_target_pairs={{0,1},{1,2},{2,3},{3,4},{4,5},{5,6},{6,7},{7,8},{8,9},{9,10},{10,1... | collective-permute-start | bytes 1769480 | tf_op jit(solution)/shard_map/ppermute | solution.py:25
  5.1 8.8 %collective-permute-start.1 = (bf16[256,1152]{1,0:T(8,128)(2,1)}, bf16[256,1152]{1,0:T(8,128)(2,1)S(1)}, u32[]{:S(2)}, u32[]{:S(2)}) collective-permute-start(bf16[256,1152]{1,0:T(8,128)(2,1)} %image_ref.2), channel_id=1, source_target_pairs={{0,30},{1,31},{2,0},{3,1},{4,2},{5,3},{6,4},{7,5},{8,6},{9,7},{10,... | collective-permute-start | bytes 1769480 | tf_op jit(solution)/shard_map/ppermute | solution.py:25
  15.3 0.1 pad_maximum_fusion.scale_ref
  15.4 1.7 %copy-done = bf16[1152,1152]{1,0:T(8,128)(2,1)S(1)} copy-done((bf16[1152,1152]{1,0:T(8,128)(2,1)S(1)}, bf16[1152,1152]{1,0:T(8,128)(2,1)}, u32[]{:S(2)}) %copy-start) | copy-done | bytes 2654232
  17.1 1.1 %copy-done.4 = bf16[256,1152]{1,0:T(8,128)(2,1)S(1)} copy-done((bf16[256,1152]{1,0:T(8,128)(2,1)S(1)}, bf16[256,1152]{1,0:T(8,128)(2,1)}, u32[]{:S(2)}) %copy-start.4) | copy-done | bytes 589848
  18.2 1.1 %copy-done.12 = bf16[256,1152]{1,0:T(8,128)(2,1)S(1)} copy-done((bf16[256,1152]{1,0:T(8,128)(2,1)S(1)}, bf16[256,1152]{1,0:T(8,128)(2,1)}, u32[]{:S(2)}) %copy-start.12) | copy-done | bytes 589848
  19.3 1.1 %copy-done.13 = s32[1152,1]{1,0:T(8,128)S(1)} copy-done((s32[1152,1]{1,0:T(8,128)S(1)}, s32[1152,1]{1,0:T(8,128)}, u32[]{:S(2)}) %copy-start.13) | copy-done | bytes 4632
  20.3 4.0 %own_blocks.1 = (bf16[1152,1280]{1,0:T(8,128)(2,1)S(1)}, bf16[256,1280]{1,0:T(8,128)(2,1)S(1)}, f32[256,1152]{1,0:T(8,128)S(1)}, f32[256,1]{1,0:T(8,128)S(1)}, b...) custom-call(f32[2]{0:T(128)S(1)} %pad_maximum_fusion.scale_ref, ...), custom_call_target="tpu_custom_call" | custom-call | flops 1736441856 | bytes 8388608 | tf_op jit(solution)/shard_map/own_blocks/pallas_call | solution.py:153
  24.4 0.0 copy-start.2
  24.4 0.0 copy-start.6
  24.4 0.0 collective-permute-done.visit_ref
  24.4 2.4 %collective-permute-done.1.image_ref = bf16[256,1152]{1,0:T(8,128)(2,1)S(1)} collective-permute-done((bf16[256,1152]{1,0:T(8,128)(2,1)}, bf16[256,1152]{1,0:T(8,128)(2,1)S(1)}, u32[]{:S(2)}, u32[]{:S(2)}) %collective-permute-start.1) | collective-permute-done | bytes 589856 | tf_op jit(solution)/shard_map/ppermute | solution.py:25
  26.9 5.3 %arrived.1 = (bf16[256,1152]{1,0:T(8,128)(2,1)}, bf16[256,1152]{1,0:T(8,128)(2,1)S(1)}, bf16[256,256]{1,0:T(8,128)(2,1)S(1)}, bf16[256,256]{1,0:T(8,128)(2,1)S(1...) custom-call(s32[1]{0:T(128)} %bitcast.core_ref, ...), custom_call_target="tpu_custom_call" | custom-call | flops 2340421632 | bytes 8388608 | tf_op jit(solution)/shard_map/arrived/pallas_call | solution.py:153
  32.2 0.0 copy-done.2
  32.2 0.0 copy-done.6
  32.2 0.0 copy-start.10
  32.2 1.5 %head_product.2 = bf16[8,2,328,128]{3,2,1,0:T(8,128)(2,1)S(1)} custom-call(bf16[576,512]{1,0:T(8,128)(2,1)S(1)} %get-tuple-element.44.back_ref, bf16[256,1280]{1,0:T(8,128)(2,1)S(1)} %get-tuple-element.42.feat_ref, bf16[256,1280]{1,0:T(8,128)(2,1)S(1)} %get-tuple-element.43.visit_ref), custom_call_target="tpu_custom_call" | custom-call | flops 754974720 | bytes 4194304 | tf_op jit(solution)/shard_map/head_product/pallas_call | solution.py:211
  33.7 0.0 copy-done.8
  33.7 0.0 copy-done.10
  33.7 1.9 %collective-permute-start.2 = (bf16[8,2,328,128]{3,2,1,0:T(8,128)(2,1)S(1)}, bf16[8,2,328,128]{3,2,1,0:T(8,128)(2,1)S(1)}, u32[]{:S(2)}, u32[]{:S(2)}) collective-permute-start(bf16[8,2,328,128]{3,2,1,0:T(8,128)(2,1)S(1)} %head_product.2), channel_id=1, source_target_pairs={{0,32},{32,0},{64,96},{96,64},{128,160},{160,128},{192,224},{224,1... | collective-permute-start | bytes 4030472 | tf_op jit(solution)/shard_map/ppermute | solution.py:339
  35.6 5.1 %collective-permute-start.3 = (bf16[256,1152]{1,0:T(8,128)(2,1)}, bf16[256,1152]{1,0:T(8,128)(2,1)}, u32[]{:S(2)}, u32[]{:S(2)}) collective-permute-start(bf16[256,1152]{1,0:T(8,128)(2,1)} %get-tuple-element.50), channel_id=1, source_target_pairs={{0,31},{1,0},{2,1},{3,2},{4,3},{5,4},{6,5},{7,6},{8,7},{9,8},{10,9... | collective-permute-start | bytes 1769480 | tf_op jit(solution)/shard_map/ppermute | solution.py:25
  40.8 0.0 collective-permute-done.2.rest_0_
  40.8 2.3 %head_product.3 = bf16[8,2,328,128]{3,2,1,0:T(8,128)(2,1)} custom-call(bf16[576,512]{1,0:T(8,128)(2,1)S(1)} %get-tuple-element.41.back_ref, bf16[256,1280]{1,0:T(8,128)(2,1)S(1)} %get-tuple-element.42.feat_ref, bf16[256,1280]{1,0:T(8,128)(2,1)S(1)} %get-tuple-element.43.visit_ref, bf16[8,2,328,128]{3,2,1,0:T(8,128)(2,1)S(1)} %collective-permute-done.2.rest_0_), custom_call_target="tpu_custom_call" | custom-call | flops 754974720 | bytes 4194304 | tf_op jit(solution)/shard_map/head_product/pallas_call | solution.py:211
  43.1 7.8 %all-to-all-start = ((bf16[16,328,128]{2,1,0:T(8,128)(2,1)}), bf16[16,328,128]{2,1,0:T(8,128)(2,1)S(1)}, u32[]{:S(2)}, u32[]{:S(2)}) async-start(bf16[16,328,128]{2,1,0:T(8,128)(2,1)} %bitcast.1), calls=%async_computation | async-start | bytes 2686976 | tf_op jit(solution)/shard_map/all_to_all | solution.py:356
  50.9 0.4 fusion.2
  51.3 0.0 copy-start.3
  51.3 0.0 copy-start.11
  51.3 1.2 %fusion = bf16[256,1152]{1,0:T(8,128)(2,1)} fusion(f32[256,1152]{1,0:T(8,128)S(1)} %fusion.2, bf16[256,256]{1,0:T(8,128)(2,1)S(1)} %get-tuple-element.53, bf16[256,1152]{1,0:T(8,128)(2,1)S(1)} %get-tuple-element.47), kind=kOutput, calls=%fused_computation.2 | convolution fusion | flops 151584768 | bytes 2490368 | tf_op jit(solution)/shard_map/dot_general | solution.py:42
  52.5 2.0 %collective-permute-start.4 = (bf16[256,1152]{1,0:T(8,128)(2,1)}, bf16[256,1152]{1,0:T(8,128)(2,1)}, u32[]{:S(2)}, u32[]{:S(2)}) collective-permute-start(bf16[256,1152]{1,0:T(8,128)(2,1)} %fusion), channel_id=1, source_target_pairs={{0,2},{1,3},{2,4},{3,5},{4,6},{5,7},{6,8},{7,9},{8,10},{9,11},{10,... | collective-permute-start | bytes 1769480 | tf_op jit(solution)/shard_map/ppermute | solution.py:25
  54.5 1.6 %collective-permute-done.3.home_ref = bf16[256,1152]{1,0:T(8,128)(2,1)} collective-permute-done((bf16[256,1152]{1,0:T(8,128)(2,1)}, bf16[256,1152]{1,0:T(8,128)(2,1)}, u32[]{:S(2)}, u32[]{:S(2)}) %collective-permute-start.3) | collective-permute-done | bytes 589856 | tf_op jit(solution)/shard_map/ppermute | solution.py:25
  56.2 0.0 copy-done.11
  56.2 1.5 %text_back.1 = bf16[256,1152]{1,0:T(8,128)(2,1)S(1)} custom-call(f32[256,1152]{1,0:T(8,128)S(1)} %copy-done.11, bf16[256,1152]{1,0:T(8,128)(2,1)} %collective-permute-done.3.home_ref, f32[256,1152]{1,0:T(8,128)S(1)} %copy-done.3, f32[256,1]{1,0:T(8,128)S(1)} %get-tuple-element.35.scale_col_ref), custom_call_target="tpu_custom_call" | custom-call | flops 20000000000 | bytes 4194304 | tf_op jit(solution)/shard_map/text_back/pallas_call | solution.py:282
  57.6 0.0 copy-start.14
  57.7 0.4 fusion.1
  58.0 0.4 copy-done.14
  58.5 0.4 convolution_add_fusion.1.own_ref
  58.8 0.0 copy-start.5
  58.8 15.0 %all-to-all-done.parts_ref = bf16[16,328,128]{2,1,0:T(8,128)(2,1)S(1)} async-done(((bf16[16,328,128]{2,1,0:T(8,128)(2,1)}), bf16[16,328,128]{2,1,0:T(8,128)(2,1)S(1)}, u32[]{:S(2)}, u32[]{:S(2)}) %all-to-all-start) | async-done | bytes 1343520 | tf_op jit(solution)/shard_map/all_to_all | solution.py:356
  73.9 0.9 sum_x_y.1
  74.8 10.2 %all-to-all-start.1 = ((bf16[16,24,128]{2,1,0:T(8,128)(2,1)}), bf16[16,24,128]{2,1,0:T(8,128)(2,1)S(1)}, u32[]{:S(2)}, u32[]{:S(2)}) async-start(bf16[16,24,128]{2,1,0:T(8,128)(2,1)} %sum_x_y.1), calls=%async_computation.1 | async-start | bytes 196608 | tf_op jit(solution)/shard_map/all_to_all | solution.py:369
  85.0 0.0 copy-start.1
  85.0 0.0 copy-start.15
  85.0 0.0 collective-permute-done.4.home_ref
  85.0 2.5 %grad_image.1 = f32[256,1152]{1,0:T(8,128)} custom-call(f32[256,1152]{1,0:T(8,128)S(1)} %convolution_add_fusion.1.own_ref, bf16[256,1152]{1,0:T(8,128)(2,1)} %collective-permute-done.4.home_ref, bf16[256,1152]{1,0:T(8,128)(2,1)S(1)} %copy-done.5), custom_call_target="tpu_custom_call" | custom-call | flops 2359296 | bytes 4194304 | tf_op jit(solution)/shard_map/grad_image/pallas_call | solution.py:282
  87.6 0.0 copy-done.15
  87.6 2.1 %fusion.3 = f32[256,1152]{1,0:T(8,128)} fusion(bf16[256,1152]{1,0:T(8,128)(2,1)S(1)} %copy-done.15, bf16[1152,1152]{1,0:T(8,128)(2,1)S(1)} %copy-done.1), kind=kOutput, calls=%fused_computation.6 | convolution fusion | flops 679477248 | bytes 4423680 | tf_op jit(solution)/shard_map/dot_general | solution.py:38
  89.6 8.7 %all-to-all-done.1.parts_ref = bf16[16,24,128]{2,1,0:T(8,128)(2,1)S(1)} async-done(((bf16[16,24,128]{2,1,0:T(8,128)(2,1)}), bf16[16,24,128]{2,1,0:T(8,128)(2,1)S(1)}, u32[]{:S(2)}, u32[]{:S(2)}) %all-to-all-start.1) | async-done | bytes 98336 | tf_op jit(solution)/shard_map/all_to_all | solution.py:369
  98.3 0.8 sum_z.1
  (12 shorter events, 0.0 us)
Async XLA Ops:
  0.6 23.8 %collective-permute-start = (bf16[256,1152]{1,0:T(8,128)(2,1)}, bf16[256,1152]{1,0:T(8,128)(2,1)S(1)}, u32[]{:S(2)}, u32[]{:S(2)}) collective-permute-start(bf16[256,1152]{1,0:T(8,128)(2,1)} %feat_ref.1), channel_id=1, source_target_pairs={{0,1},{1,2},{2,3},{3,4},{4,5},{5,6},{6,7},{7,8},{8,9},{9,10},{10,1... | collective-permute-start | bytes 1769480 | tf_op jit(solution)/shard_map/ppermute | solution.py:25
  5.1 21.7 %collective-permute-start.1 = (bf16[256,1152]{1,0:T(8,128)(2,1)}, bf16[256,1152]{1,0:T(8,128)(2,1)S(1)}, u32[]{:S(2)}, u32[]{:S(2)}) collective-permute-start(bf16[256,1152]{1,0:T(8,128)(2,1)} %image_ref.2), channel_id=1, source_target_pairs={{0,30},{1,31},{2,0},{3,1},{4,2},{5,3},{6,4},{7,5},{8,6},{9,7},{10,... | collective-permute-start | bytes 1769480 | tf_op jit(solution)/shard_map/ppermute | solution.py:25
  15.4 1.8 %copy-start = (bf16[1152,1152]{1,0:T(8,128)(2,1)S(1)}, bf16[1152,1152]{1,0:T(8,128)(2,1)}, u32[]{:S(2)}) copy-start(bf16[1152,1152]{1,0:T(8,128)(2,1)} %head_ref.3) | copy-start | bytes 7962628
  17.1 1.1 %copy-start.4 = (bf16[256,1152]{1,0:T(8,128)(2,1)S(1)}, bf16[256,1152]{1,0:T(8,128)(2,1)}, u32[]{:S(2)}) copy-start(bf16[256,1152]{1,0:T(8,128)(2,1)} %image_ref.2) | copy-start | bytes 1769476
  18.2 1.1 %copy-start.12 = (bf16[256,1152]{1,0:T(8,128)(2,1)S(1)}, bf16[256,1152]{1,0:T(8,128)(2,1)}, u32[]{:S(2)}) copy-start(bf16[256,1152]{1,0:T(8,128)(2,1)} %feat_ref.1) | copy-start | bytes 1769476
  19.3 1.1 %copy-start.13 = (s32[1152,1]{1,0:T(8,128)S(1)}, s32[1152,1]{1,0:T(8,128)}, u32[]{:S(2)}) copy-start(s32[1152,1]{1,0:T(8,128)} %constant.21.clone.target_ref) | copy-start | bytes 13828
  24.4 7.8 %copy-start.2 = (f32[256,1152]{1,0:T(8,128)}, f32[256,1152]{1,0:T(8,128)S(1)}, u32[]{:S(2)}) copy-start(f32[256,1152]{1,0:T(8,128)S(1)} %get-tuple-element.34.unit_ref) | copy-start | bytes 3538948
  24.4 7.8 %copy-start.6 = (bf16[256,256]{1,0:T(8,128)(2,1)}, bf16[256,256]{1,0:T(8,128)(2,1)S(1)}, u32[]{:S(2)}) copy-start(bf16[256,256]{1,0:T(8,128)(2,1)S(1)} %get-tuple-element.45) | copy-start | bytes 393220
  32.2 1.5 %copy-start.8 = (bf16[256,256]{1,0:T(8,128)(2,1)}, bf16[256,256]{1,0:T(8,128)(2,1)S(1)}, u32[]{:S(2)}) copy-start(bf16[256,256]{1,0:T(8,128)(2,1)S(1)} %get-tuple-element.52) | copy-start | bytes 393220
  32.2 1.5 %copy-start.10 = (f32[256,1152]{1,0:T(8,128)}, f32[256,1152]{1,0:T(8,128)S(1)}, u32[]{:S(2)}) copy-start(f32[256,1152]{1,0:T(8,128)S(1)} %get-tuple-element.48.own_ref) | copy-start | bytes 3538948
  33.7 7.1 %collective-permute-start.2 = (bf16[8,2,328,128]{3,2,1,0:T(8,128)(2,1)S(1)}, bf16[8,2,328,128]{3,2,1,0:T(8,128)(2,1)S(1)}, u32[]{:S(2)}, u32[]{:S(2)}) collective-permute-start(bf16[8,2,328,128]{3,2,1,0:T(8,128)(2,1)S(1)} %head_product.2), channel_id=1, source_target_pairs={{0,32},{32,0},{64,96},{96,64},{128,160},{160,128},{192,224},{224,1... | collective-permute-start | bytes 4030472 | tf_op jit(solution)/shard_map/ppermute | solution.py:339
  35.6 20.5 %collective-permute-start.3 = (bf16[256,1152]{1,0:T(8,128)(2,1)}, bf16[256,1152]{1,0:T(8,128)(2,1)}, u32[]{:S(2)}, u32[]{:S(2)}) collective-permute-start(bf16[256,1152]{1,0:T(8,128)(2,1)} %get-tuple-element.50), channel_id=1, source_target_pairs={{0,31},{1,0},{2,1},{3,2},{4,3},{5,4},{6,5},{7,6},{8,7},{9,8},{10,9... | collective-permute-start | bytes 1769480 | tf_op jit(solution)/shard_map/ppermute | solution.py:25
  43.1 7.8 %copy-start.9 = (bf16[256,256]{1,0:T(8,128)(2,1)S(1)}, bf16[256,256]{1,0:T(8,128)(2,1)}, u32[]{:S(2)}) copy-start(bf16[256,256]{1,0:T(8,128)(2,1)} %copy-done.8) | copy-start | bytes 393220
  43.1 30.8 %all-to-all-start = ((bf16[16,328,128]{2,1,0:T(8,128)(2,1)}), bf16[16,328,128]{2,1,0:T(8,128)(2,1)S(1)}, u32[]{:S(2)}, u32[]{:S(2)}) async-start(bf16[16,328,128]{2,1,0:T(8,128)(2,1)} %bitcast.1), calls=%async_computation | async-start | bytes 2686976 | tf_op jit(solution)/shard_map/all_to_all | solution.py:356
  51.3 4.9 %copy-start.3 = (f32[256,1152]{1,0:T(8,128)S(1)}, f32[256,1152]{1,0:T(8,128)}, u32[]{:S(2)}) copy-start(f32[256,1152]{1,0:T(8,128)} %copy-done.2) | copy-start | bytes 3538948
  51.3 4.9 %copy-start.11 = (f32[256,1152]{1,0:T(8,128)S(1)}, f32[256,1152]{1,0:T(8,128)}, u32[]{:S(2)}) copy-start(f32[256,1152]{1,0:T(8,128)} %copy-done.10) | copy-start | bytes 3538948
  52.5 5.2 %copy-start.7 = (bf16[256,256]{1,0:T(8,128)(2,1)S(1)}, bf16[256,256]{1,0:T(8,128)(2,1)}, u32[]{:S(2)}) copy-start(bf16[256,256]{1,0:T(8,128)(2,1)} %copy-done.6) | copy-start | bytes 393220
  52.5 32.5 %collective-permute-start.4 = (bf16[256,1152]{1,0:T(8,128)(2,1)}, bf16[256,1152]{1,0:T(8,128)(2,1)}, u32[]{:S(2)}, u32[]{:S(2)}) collective-permute-start(bf16[256,1152]{1,0:T(8,128)(2,1)} %fusion), channel_id=1, source_target_pairs={{0,2},{1,3},{2,4},{3,5},{4,6},{5,7},{6,8},{7,9},{8,10},{9,11},{10,... | collective-permute-start | bytes 1769480 | tf_op jit(solution)/shard_map/ppermute | solution.py:25
  57.6 0.8 copy-start.14
  58.8 26.2 %copy-start.5 = (bf16[256,1152]{1,0:T(8,128)(2,1)S(1)}, bf16[256,1152]{1,0:T(8,128)(2,1)}, u32[]{:S(2)}) copy-start(bf16[256,1152]{1,0:T(8,128)(2,1)} %image_ref.2) | copy-start | bytes 1769476
  74.8 23.5 %all-to-all-start.1 = ((bf16[16,24,128]{2,1,0:T(8,128)(2,1)}), bf16[16,24,128]{2,1,0:T(8,128)(2,1)S(1)}, u32[]{:S(2)}, u32[]{:S(2)}) async-start(bf16[16,24,128]{2,1,0:T(8,128)(2,1)} %sum_x_y.1), calls=%async_computation.1 | async-start | bytes 196608 | tf_op jit(solution)/shard_map/all_to_all | solution.py:369
  85.0 2.6 %copy-start.1 = (bf16[1152,1152]{1,0:T(8,128)(2,1)S(1)}, bf16[1152,1152]{1,0:T(8,128)(2,1)}, u32[]{:S(2)}) copy-start(bf16[1152,1152]{1,0:T(8,128)(2,1)} %head_ref.3) | copy-start | bytes 7962628
  85.0 2.6 %copy-start.15 = (bf16[256,1152]{1,0:T(8,128)(2,1)S(1)}, bf16[256,1152]{1,0:T(8,128)(2,1)}, u32[]{:S(2)}) copy-start(bf16[256,1152]{1,0:T(8,128)(2,1)} %copy-done.14) | copy-start | bytes 1769476

commit v2 on v1

--- a/solution.py
+++ b/solution.py
@@ -192,14 +192,16 @@
     share = back_ref.shape[0] // (NX * NYL)
     used = back_ref.shape[0] * NC // NYH
     half = feat_ref.shape[1] // NYH
-    lanes = pl.ds(pl.multiple_of(pl.program_id(0) * half, LANES), half)
-    total = dot_nn(back_ref[:, :rows], feat_ref[:, lanes])
-    total += dot_nn(back_ref[:, rows:], visit_ref[:, lanes])
-    for part in range(NX * NYL):
-        cut = in_tiles(total[part * share : (part + 1) * share, :used])
-        if len(rest) > 1:
-            cut += rest[0][part, pl.program_id(0)].astype(jnp.float32)
-        out_ref[part, 0] = cut.astype(jnp.bfloat16)
+    for yh in range(NYH):
+        lanes = slice(yh * half, (yh + 1) * half)
+        total = dot_nn(back_ref[:, :rows], feat_ref[:, lanes])
+        total += dot_nn(back_ref[:, rows:], visit_ref[:, lanes])
+        for part in range(NX * NYL):
+            peer = (part // NYL * NYH + yh) * NYL + part % NYL
+            cut = in_tiles(total[part * share : (part + 1) * share, :used])
+            if len(rest) > 1:
+                cut += rest[0][peer].astype(jnp.float32)
+            out_ref[peer] = cut.astype(jnp.bfloat16)
 
 
 def head_product(back, feat, visit, *added):
@@ -207,13 +209,12 @@
     width = feat.shape[1]
     parts = NX * NYL
     share, used = cols // parts, cols * NC // NYH
-    high = used // LANES * share + tail_rows(share)
+    shape = (parts * NYH, used // LANES * share + tail_rows(share), LANES)
     return pl.pallas_call(
         product_kernel,
-        grid=(NYH,),
         in_specs=[VMEM] * (3 + len(added)),
-        out_specs=pl.BlockSpec((parts, 1, high, LANES), lambda i: (0, i, 0, 0)),
-        out_shape=jax.ShapeDtypeStruct((parts, NYH, high, LANES), jnp.bfloat16),
+        out_specs=VMEM,
+        out_shape=jax.ShapeDtypeStruct(shape, jnp.bfloat16),
         compiler_params=LIMIT,
         cost_estimate=pl.CostEstimate(flops=2 * cols * rows * width, bytes_accessed=4 << 20, transcendentals=0),
         name="head_product",
@@ -340,13 +341,12 @@
     text_part, _ = lax.optimization_barrier((text_part, head_other))
     text_home = shifted(text_part, 0, -1)
     head_part = head_product(back_mine, feat_sorted, visit_sorted, head_in)
-    head_part = head_part.reshape(-1, *head_part.shape[2:])
     groups = [
         [
             ((x * NYL + yl) * NC + c) * N_DY + z * NYH + yh
             for x in range(NX)
+            for yh in range(NYH)
             for yl in range(NYL)
-            for yh in range(NYH)
         ]
         for c in range(NC)
         for z in range(NZ)

time: 99.7 us -> 97.5 us (0.978)
  waiting for transfers between devices: 27.8 us -> 26 us
    all_to_all x1, waiting for transfers between devices: 15 us -> 12.4 us  [local(): lax.all_to_all(head_part, ('dx', 'dy'), 0, 0, axis_index_groups=groups, t...]
    unnamed x32 -> x24, local copies, waits for them, and re-layouts: 5.44 us -> 5.42 us
  transfers between devices with their start and end apart: 7 -> 7, of which waited for: 4 -> 4; matrix products, arithmetic and copies ran while one was open for 4% -> 5% of each run, Pallas kernels for 11% -> 12%
where the time goes in v2:
time: 97.5 us; the launch traced here: 96.9 us
  starting transfers between devices  40.4 us (41%)
  waiting for transfers between devices  26 us (27%)
  Pallas kernels  18.4 us (19%)
  local copies, waits for them, and re-layouts  5.42 us (6%)
  matrix products  4.38 us (4%)
  between operations  2.15 us (2%)
    ppermute x4, starting transfers between devices, shifted(): return lax.ppermute(value, 'dy', pairs)  20.4 us
    all_to_all x1, waiting for transfers between devices, local(): lax.all_to_all(head_part, ('dx', 'dy'), 0, 0, axis_index_groups=groups, t...  12.4 us
    all_to_all x1, starting transfers between devices, local(): lax.all_to_all(head_part, 'dy', 0, 0, axis_index_groups=groups, tiled=True)  10.5 us
    pallas_call x2, Pallas kernels, in_vmem(): pl.pallas_call(kernel, in_specs=[SMEM] * len(scalars) + [VMEM] * len(arra...  9.35 us
    all_to_all x1, waiting for transfers between devices, local(): lax.all_to_all(head_part, 'dy', 0, 0, axis_index_groups=groups, tiled=True)  9.19 us
    all_to_all x1, starting transfers between devices, local(): lax.all_to_all(head_part, ('dx', 'dy'), 0, 0, axis_index_groups=groups, t...  7.63 us
    unnamed x24, local copies, waits for them, and re-layouts  5.42 us
    ppermute x4, waiting for transfers between devices, shifted(): return lax.ppermute(value, 'dy', pairs)  4.44 us
  transfers between devices with their start and end apart: 7, of which 4 were waited for; matrix products, arithmetic and copies ran while one was open for 5% of the time, Pallas kernels for 12%

profile of v2, /device:TPU:24, one launch (start us, length us, event | category | flops | bytes accessed | tf_op | source)
XLA Modules:
  0.0 96.9 jit_solution(6650358894502925122)
XLA Ops:
  0.6 4.5 %collective-permute-start = (bf16[256,1152]{1,0:T(8,128)(2,1)}, bf16[256,1152]{1,0:T(8,128)(2,1)S(1)}, u32[]{:S(2)}, u32[]{:S(2)}) collective-permute-start(bf16[256,1152]{1,0:T(8,128)(2,1)} %feat_ref.1), channel_id=1, source_target_pairs={{0,1},{1,2},{2,3},{3,4},{4,5},{5,6},{6,7},{7,8},{8,9},{9,10},{10,1... | collective-permute-start | bytes 1769480 | tf_op jit(solution)/shard_map/ppermute | solution.py:25
  5.1 8.8 %collective-permute-start.1 = (bf16[256,1152]{1,0:T(8,128)(2,1)}, bf16[256,1152]{1,0:T(8,128)(2,1)S(1)}, u32[]{:S(2)}, u32[]{:S(2)}) collective-permute-start(bf16[256,1152]{1,0:T(8,128)(2,1)} %image_ref.2), channel_id=1, source_target_pairs={{0,30},{1,31},{2,0},{3,1},{4,2},{5,3},{6,4},{7,5},{8,6},{9,7},{10,... | collective-permute-start | bytes 1769480 | tf_op jit(solution)/shard_map/ppermute | solution.py:25
  15.3 0.1 pad_maximum_fusion.scale_ref
  15.4 0.0 copy-start
  15.4 1.7 %copy-done = bf16[1152,1152]{1,0:T(8,128)(2,1)S(1)} copy-done((bf16[1152,1152]{1,0:T(8,128)(2,1)S(1)}, bf16[1152,1152]{1,0:T(8,128)(2,1)}, u32[]{:S(2)}) %copy-start) | copy-done | bytes 2654232
  17.1 1.1 %copy-done.4 = bf16[256,1152]{1,0:T(8,128)(2,1)S(1)} copy-done((bf16[256,1152]{1,0:T(8,128)(2,1)S(1)}, bf16[256,1152]{1,0:T(8,128)(2,1)}, u32[]{:S(2)}) %copy-start.4) | copy-done | bytes 589848
  18.2 1.1 %copy-done.8 = bf16[256,1152]{1,0:T(8,128)(2,1)S(1)} copy-done((bf16[256,1152]{1,0:T(8,128)(2,1)S(1)}, bf16[256,1152]{1,0:T(8,128)(2,1)}, u32[]{:S(2)}) %copy-start.8) | copy-done | bytes 589848
  19.3 1.1 %copy-done.9 = s32[1152,1]{1,0:T(8,128)S(1)} copy-done((s32[1152,1]{1,0:T(8,128)S(1)}, s32[1152,1]{1,0:T(8,128)}, u32[]{:S(2)}) %copy-start.9) | copy-done | bytes 4632
  20.3 4.0 %own_blocks.1 = (bf16[1152,1280]{1,0:T(8,128)(2,1)S(1)}, bf16[256,1280]{1,0:T(8,128)(2,1)S(1)}, f32[256,1152]{1,0:T(8,128)S(1)}, f32[256,1]{1,0:T(8,128)S(1)}, b...) custom-call(f32[2]{0:T(128)S(1)} %pad_maximum_fusion.scale_ref, ...), custom_call_target="tpu_custom_call" | custom-call | flops 1736441856 | bytes 8388608 | tf_op jit(solution)/shard_map/own_blocks/pallas_call | solution.py:153
  24.4 0.0 copy-start.2
  24.4 0.0 collective-permute-done.visit_ref
  24.4 2.5 %collective-permute-done.1.image_ref = bf16[256,1152]{1,0:T(8,128)(2,1)S(1)} collective-permute-done((bf16[256,1152]{1,0:T(8,128)(2,1)}, bf16[256,1152]{1,0:T(8,128)(2,1)S(1)}, u32[]{:S(2)}, u32[]{:S(2)}) %collective-permute-start.1) | collective-permute-done | bytes 589856 | tf_op jit(solution)/shard_map/ppermute | solution.py:25
  26.9 5.3 %arrived.1 = (bf16[256,1152]{1,0:T(8,128)(2,1)}, bf16[256,1152]{1,0:T(8,128)(2,1)S(1)}, bf16[256,256]{1,0:T(8,128)(2,1)S(1)}, bf16[256,256]{1,0:T(8,128)(2,1)S(1...) custom-call(s32[1]{0:T(128)} %bitcast.core_ref, ...), custom_call_target="tpu_custom_call" | custom-call | flops 2340421632 | bytes 8388608 | tf_op jit(solution)/shard_map/arrived/pallas_call | solution.py:153
  32.2 0.0 copy-done.2
  32.2 1.2 %head_product.2 = bf16[16,328,128]{2,1,0:T(8,128)(2,1)S(1)} custom-call(bf16[576,512]{1,0:T(8,128)(2,1)S(1)} %get-tuple-element.44.back_ref, bf16[256,1280]{1,0:T(8,128)(2,1)S(1)} %get-tuple-element.42.feat_ref, bf16[256,1280]{1,0:T(8,128)(2,1)S(1)} %get-tuple-element.43.visit_ref), custom_call_target="tpu_custom_call" | custom-call | flops 754974720 | bytes 4194304 | tf_op jit(solution)/shard_map/head_product/pallas_call | solution.py:213
  33.3 0.0 copy-done.6
  33.3 1.9 %collective-permute-start.2 = (bf16[16,328,128]{2,1,0:T(8,128)(2,1)S(1)}, bf16[16,328,128]{2,1,0:T(8,128)(2,1)S(1)}, u32[]{:S(2)}, u32[]{:S(2)}) collective-permute-start(bf16[16,328,128]{2,1,0:T(8,128)(2,1)S(1)} %head_product.2), channel_id=1, source_target_pairs={{0,32},{32,0},{64,96},{96,64},{128,160},{160,128},{192,224},{224,1... | collective-permute-start | bytes 4030472 | tf_op jit(solution)/shard_map/ppermute | solution.py:340
  35.3 5.1 %collective-permute-start.3 = (bf16[256,1152]{1,0:T(8,128)(2,1)}, bf16[256,1152]{1,0:T(8,128)(2,1)}, u32[]{:S(2)}, u32[]{:S(2)}) collective-permute-start(bf16[256,1152]{1,0:T(8,128)(2,1)} %get-tuple-element.50), channel_id=1, source_target_pairs={{0,31},{1,0},{2,1},{3,2},{4,3},{5,4},{6,5},{7,6},{8,7},{9,8},{10,9... | collective-permute-start | bytes 1769480 | tf_op jit(solution)/shard_map/ppermute | solution.py:25
  40.4 0.0 collective-permute-done.2.rest_0_
  40.4 2.3 %head_product.3 = bf16[16,328,128]{2,1,0:T(8,128)(2,1)} custom-call(bf16[576,512]{1,0:T(8,128)(2,1)S(1)} %get-tuple-element.41.back_ref, bf16[256,1280]{1,0:T(8,128)(2,1)S(1)} %get-tuple-element.42.feat_ref, bf16[256,1280]{1,0:T(8,128)(2,1)S(1)} %get-tuple-element.43.visit_ref, bf16[16,328,128]{2,1,0:T(8,128)(2,1)S(1)} %collective-permute-done.2.rest_0_), custom_call_target="tpu_custom_call" | custom-call | flops 754974720 | bytes 4194304 | tf_op jit(solution)/shard_map/head_product/pallas_call | solution.py:213
  42.7 7.6 %all-to-all-start = ((bf16[16,328,128]{2,1,0:T(8,128)(2,1)}), bf16[16,328,128]{2,1,0:T(8,128)(2,1)S(1)}, u32[]{:S(2)}, u32[]{:S(2)}) async-start(bf16[16,328,128]{2,1,0:T(8,128)(2,1)} %head_product.3), calls=%async_computation | async-start | bytes 2686976 | tf_op jit(solution)/shard_map/all_to_all | solution.py:356
  50.3 0.4 fusion.2
  50.7 0.0 copy-start.3
  50.7 0.0 copy-start.7
  50.7 1.2 %fusion = bf16[256,1152]{1,0:T(8,128)(2,1)} fusion(f32[256,1152]{1,0:T(8,128)S(1)} %fusion.2, bf16[256,256]{1,0:T(8,128)(2,1)S(1)} %get-tuple-element.52, bf16[256,1152]{1,0:T(8,128)(2,1)S(1)} %get-tuple-element.33.text_low_ref), kind=kOutput, calls=%fused_computation.2 | convolution fusion | flops 151584768 | bytes 2490368 | tf_op jit(solution)/shard_map/dot_general | solution.py:42
  51.9 1.9 %collective-permute-start.4 = (bf16[256,1152]{1,0:T(8,128)(2,1)}, bf16[256,1152]{1,0:T(8,128)(2,1)}, u32[]{:S(2)}, u32[]{:S(2)}) collective-permute-start(bf16[256,1152]{1,0:T(8,128)(2,1)} %fusion), channel_id=1, source_target_pairs={{0,2},{1,3},{2,4},{3,5},{4,6},{5,7},{6,8},{7,9},{8,10},{9,11},{10,... | collective-permute-start | bytes 1769480 | tf_op jit(solution)/shard_map/ppermute | solution.py:25
  53.8 2.0 %collective-permute-done.3.home_ref = bf16[256,1152]{1,0:T(8,128)(2,1)} collective-permute-done((bf16[256,1152]{1,0:T(8,128)(2,1)}, bf16[256,1152]{1,0:T(8,128)(2,1)}, u32[]{:S(2)}, u32[]{:S(2)}) %collective-permute-start.3) | collective-permute-done | bytes 589856 | tf_op jit(solution)/shard_map/ppermute | solution.py:25
  55.8 0.0 copy-done.3
  55.8 0.0 copy-done.7
  55.8 1.5 %text_back.1 = bf16[256,1152]{1,0:T(8,128)(2,1)S(1)} custom-call(f32[256,1152]{1,0:T(8,128)S(1)} %copy-done.7, bf16[256,1152]{1,0:T(8,128)(2,1)} %collective-permute-done.3.home_ref, f32[256,1152]{1,0:T(8,128)S(1)} %copy-done.3, f32[256,1]{1,0:T(8,128)S(1)} %get-tuple-element.35.scale_col_ref), custom_call_target="tpu_custom_call" | custom-call | flops 20000000000 | bytes 4194304 | tf_op jit(solution)/shard_map/text_back/pallas_call | solution.py:283
  57.3 0.0 copy-start.10
  57.3 0.4 fusion.1
  57.7 0.4 copy-done.10
  58.1 0.4 convolution_add_fusion.1.own_ref
  58.5 0.0 copy-start.5
  58.5 12.4 %all-to-all-done.parts_ref = bf16[16,328,128]{2,1,0:T(8,128)(2,1)S(1)} async-done(((bf16[16,328,128]{2,1,0:T(8,128)(2,1)}), bf16[16,328,128]{2,1,0:T(8,128)(2,1)S(1)}, u32[]{:S(2)}, u32[]{:S(2)}) %all-to-all-start) | async-done | bytes 1343520 | tf_op jit(solution)/shard_map/all_to_all | solution.py:356
  70.9 0.9 sum_x_y.1
  71.8 10.5 %all-to-all-start.1 = ((bf16[16,24,128]{2,1,0:T(8,128)(2,1)}), bf16[16,24,128]{2,1,0:T(8,128)(2,1)S(1)}, u32[]{:S(2)}, u32[]{:S(2)}) async-start(bf16[16,24,128]{2,1,0:T(8,128)(2,1)} %sum_x_y.1), calls=%async_computation.1 | async-start | bytes 196608 | tf_op jit(solution)/shard_map/all_to_all | solution.py:369
  82.3 0.0 copy-start.1
  82.3 0.0 copy-start.11
  82.3 0.0 collective-permute-done.4.home_ref
  82.3 0.0 copy-done.5
  82.3 2.5 %grad_image.1 = f32[256,1152]{1,0:T(8,128)} custom-call(f32[256,1152]{1,0:T(8,128)S(1)} %convolution_add_fusion.1.own_ref, bf16[256,1152]{1,0:T(8,128)(2,1)} %collective-permute-done.4.home_ref, bf16[256,1152]{1,0:T(8,128)(2,1)S(1)} %copy-done.5), custom_call_target="tpu_custom_call" | custom-call | flops 2359296 | bytes 4194304 | tf_op jit(solution)/shard_map/grad_image/pallas_call | solution.py:283
  84.8 0.0 copy-done.1
  84.8 0.0 copy-done.11
  84.8 2.1 %fusion.3 = f32[256,1152]{1,0:T(8,128)} fusion(bf16[256,1152]{1,0:T(8,128)(2,1)S(1)} %copy-done.11, bf16[1152,1152]{1,0:T(8,128)(2,1)S(1)} %copy-done.1), kind=kOutput, calls=%fused_computation.6 | convolution fusion | flops 679477248 | bytes 4423680 | tf_op jit(solution)/shard_map/dot_general | solution.py:38
  86.9 9.2 %all-to-all-done.1.parts_ref = bf16[16,24,128]{2,1,0:T(8,128)(2,1)S(1)} async-done(((bf16[16,24,128]{2,1,0:T(8,128)(2,1)}), bf16[16,24,128]{2,1,0:T(8,128)(2,1)S(1)}, u32[]{:S(2)}, u32[]{:S(2)}) %all-to-all-start.1) | async-done | bytes 98336 | tf_op jit(solution)/shard_map/all_to_all | solution.py:369
  96.1 0.8 sum_z.1
  (4 shorter events, 0.0 us)
Async XLA Ops:
  0.6 23.8 %collective-permute-start = (bf16[256,1152]{1,0:T(8,128)(2,1)}, bf16[256,1152]{1,0:T(8,128)(2,1)S(1)}, u32[]{:S(2)}, u32[]{:S(2)}) collective-permute-start(bf16[256,1152]{1,0:T(8,128)(2,1)} %feat_ref.1), channel_id=1, source_target_pairs={{0,1},{1,2},{2,3},{3,4},{4,5},{5,6},{6,7},{7,8},{8,9},{9,10},{10,1... | collective-permute-start | bytes 1769480 | tf_op jit(solution)/shard_map/ppermute | solution.py:25
  5.1 21.7 %collective-permute-start.1 = (bf16[256,1152]{1,0:T(8,128)(2,1)}, bf16[256,1152]{1,0:T(8,128)(2,1)S(1)}, u32[]{:S(2)}, u32[]{:S(2)}) collective-permute-start(bf16[256,1152]{1,0:T(8,128)(2,1)} %image_ref.2), channel_id=1, source_target_pairs={{0,30},{1,31},{2,0},{3,1},{4,2},{5,3},{6,4},{7,5},{8,6},{9,7},{10,... | collective-permute-start | bytes 1769480 | tf_op jit(solution)/shard_map/ppermute | solution.py:25
  15.4 1.8 %copy-start = (bf16[1152,1152]{1,0:T(8,128)(2,1)S(1)}, bf16[1152,1152]{1,0:T(8,128)(2,1)}, u32[]{:S(2)}) copy-start(bf16[1152,1152]{1,0:T(8,128)(2,1)} %head_ref.3) | copy-start | bytes 7962628
  17.1 1.1 %copy-start.4 = (bf16[256,1152]{1,0:T(8,128)(2,1)S(1)}, bf16[256,1152]{1,0:T(8,128)(2,1)}, u32[]{:S(2)}) copy-start(bf16[256,1152]{1,0:T(8,128)(2,1)} %image_ref.2) | copy-start | bytes 1769476
  18.2 1.1 %copy-start.8 = (bf16[256,1152]{1,0:T(8,128)(2,1)S(1)}, bf16[256,1152]{1,0:T(8,128)(2,1)}, u32[]{:S(2)}) copy-start(bf16[256,1152]{1,0:T(8,128)(2,1)} %feat_ref.1) | copy-start | bytes 1769476
  19.3 1.1 %copy-start.9 = (s32[1152,1]{1,0:T(8,128)S(1)}, s32[1152,1]{1,0:T(8,128)}, u32[]{:S(2)}) copy-start(s32[1152,1]{1,0:T(8,128)} %constant.21.clone.target_ref) | copy-start | bytes 13828
  24.4 7.8 %copy-start.2 = (f32[256,1152]{1,0:T(8,128)}, f32[256,1152]{1,0:T(8,128)S(1)}, u32[]{:S(2)}) copy-start(f32[256,1152]{1,0:T(8,128)S(1)} %get-tuple-element.34.unit_ref) | copy-start | bytes 3538948
  32.2 1.2 %copy-start.6 = (f32[256,1152]{1,0:T(8,128)}, f32[256,1152]{1,0:T(8,128)S(1)}, u32[]{:S(2)}) copy-start(f32[256,1152]{1,0:T(8,128)S(1)} %get-tuple-element.48.own_ref) | copy-start | bytes 3538948
  33.3 7.1 %collective-permute-start.2 = (bf16[16,328,128]{2,1,0:T(8,128)(2,1)S(1)}, bf16[16,328,128]{2,1,0:T(8,128)(2,1)S(1)}, u32[]{:S(2)}, u32[]{:S(2)}) collective-permute-start(bf16[16,328,128]{2,1,0:T(8,128)(2,1)S(1)} %head_product.2), channel_id=1, source_target_pairs={{0,32},{32,0},{64,96},{96,64},{128,160},{160,128},{192,224},{224,1... | collective-permute-start | bytes 4030472 | tf_op jit(solution)/shard_map/ppermute | solution.py:340
  35.3 20.5 %collective-permute-start.3 = (bf16[256,1152]{1,0:T(8,128)(2,1)}, bf16[256,1152]{1,0:T(8,128)(2,1)}, u32[]{:S(2)}, u32[]{:S(2)}) collective-permute-start(bf16[256,1152]{1,0:T(8,128)(2,1)} %get-tuple-element.50), channel_id=1, source_target_pairs={{0,31},{1,0},{2,1},{3,2},{4,3},{5,4},{6,5},{7,6},{8,7},{9,8},{10,9... | collective-permute-start | bytes 1769480 | tf_op jit(solution)/shard_map/ppermute | solution.py:25
  42.7 28.2 %all-to-all-start = ((bf16[16,328,128]{2,1,0:T(8,128)(2,1)}), bf16[16,328,128]{2,1,0:T(8,128)(2,1)S(1)}, u32[]{:S(2)}, u32[]{:S(2)}) async-start(bf16[16,328,128]{2,1,0:T(8,128)(2,1)} %head_product.3), calls=%async_computation | async-start | bytes 2686976 | tf_op jit(solution)/shard_map/all_to_all | solution.py:356
  50.7 5.1 %copy-start.3 = (f32[256,1152]{1,0:T(8,128)S(1)}, f32[256,1152]{1,0:T(8,128)}, u32[]{:S(2)}) copy-start(f32[256,1152]{1,0:T(8,128)} %copy-done.2) | copy-start | bytes 3538948
  50.7 5.1 %copy-start.7 = (f32[256,1152]{1,0:T(8,128)S(1)}, f32[256,1152]{1,0:T(8,128)}, u32[]{:S(2)}) copy-start(f32[256,1152]{1,0:T(8,128)} %copy-done.6) | copy-start | bytes 3538948
  51.9 30.4 %collective-permute-start.4 = (bf16[256,1152]{1,0:T(8,128)(2,1)}, bf16[256,1152]{1,0:T(8,128)(2,1)}, u32[]{:S(2)}, u32[]{:S(2)}) collective-permute-start(bf16[256,1152]{1,0:T(8,128)(2,1)} %fusion), channel_id=1, source_target_pairs={{0,2},{1,3},{2,4},{3,5},{4,6},{5,7},{6,8},{7,9},{8,10},{9,11},{10,... | collective-permute-start | bytes 1769480 | tf_op jit(solution)/shard_map/ppermute | solution.py:25
  57.3 0.8 copy-start.10
  58.5 23.8 %copy-start.5 = (bf16[256,1152]{1,0:T(8,128)(2,1)S(1)}, bf16[256,1152]{1,0:T(8,128)(2,1)}, u32[]{:S(2)}) copy-start(bf16[256,1152]{1,0:T(8,128)(2,1)} %image_ref.2) | copy-start | bytes 1769476
  71.8 24.3 %all-to-all-start.1 = ((bf16[16,24,128]{2,1,0:T(8,128)(2,1)}), bf16[16,24,128]{2,1,0:T(8,128)(2,1)S(1)}, u32[]{:S(2)}, u32[]{:S(2)}) async-start(bf16[16,24,128]{2,1,0:T(8,128)(2,1)} %sum_x_y.1), calls=%async_computation.1 | async-start | bytes 196608 | tf_op jit(solution)/shard_map/all_to_all | solution.py:369
  82.3 2.6 %copy-start.1 = (bf16[1152,1152]{1,0:T(8,128)(2,1)S(1)}, bf16[1152,1152]{1,0:T(8,128)(2,1)}, u32[]{:S(2)}) copy-start(bf16[1152,1152]{1,0:T(8,128)(2,1)} %head_ref.3) | copy-start | bytes 7962628
  82.3 2.6 %copy-start.11 = (bf16[256,1152]{1,0:T(8,128)(2,1)S(1)}, bf16[256,1152]{1,0:T(8,128)(2,1)}, u32[]{:S(2)}) copy-start(bf16[256,1152]{1,0:T(8,128)(2,1)} %copy-done.10) | copy-start | bytes 1769476

commit v3 on v2

--- a/solution.py
+++ b/solution.py
@@ -197,7 +197,7 @@
         total = dot_nn(back_ref[:, :rows], feat_ref[:, lanes])
         total += dot_nn(back_ref[:, rows:], visit_ref[:, lanes])
         for part in range(NX * NYL):
-            peer = (part // NYL * NYH + yh) * NYL + part % NYL
+            peer = (yh * NYL + part % NYL) * NX + part // NYL
             cut = in_tiles(total[part * share : (part + 1) * share, :used])
             if len(rest) > 1:
                 cut += rest[0][peer].astype(jnp.float32)
@@ -344,9 +344,9 @@
     groups = [
         [
             ((x * NYL + yl) * NC + c) * N_DY + z * NYH + yh
-            for x in range(NX)
             for yh in range(NYH)
             for yl in range(NYL)
+            for x in range(NX)
         ]
         for c in range(NC)
         for z in range(NZ)

time: 97.5 us -> 98.8 us (1.013); the launches traced: 96.9 us -> 96.9 us
    all_to_all x1, waiting for transfers between devices: 12.4 us -> 10.1 us  [local(): lax.all_to_all(head_part, ('dx', 'dy'), 0, 0, axis_index_groups=groups, t...]
    ppermute x4, waiting for transfers between devices: 4.44 us -> 6.36 us  [shifted(): return lax.ppermute(value, 'dy', pairs)]
where the time goes in v3:
time: 98.8 us; the launch traced here: 96.9 us
  starting transfers between devices  40.8 us (41%)
  waiting for transfers between devices  25.6 us (26%)
  Pallas kernels  18.4 us (19%)
  local copies, waits for them, and re-layouts  5.42 us (5%)
  matrix products  4.38 us (4%)
  between operations  2.15 us (2%)
    ppermute x4, starting transfers between devices, shifted(): return lax.ppermute(value, 'dy', pairs)  20.4 us
    all_to_all x1, starting transfers between devices, local(): lax.all_to_all(head_part, 'dy', 0, 0, axis_index_groups=groups, tiled=True)  10.9 us
    all_to_all x1, waiting for transfers between devices, local(): lax.all_to_all(head_part, ('dx', 'dy'), 0, 0, axis_index_groups=groups, t...  10.1 us
    pallas_call x2, Pallas kernels, in_vmem(): pl.pallas_call(kernel, in_specs=[SMEM] * len(scalars) + [VMEM] * len(arra...  9.35 us
    all_to_all x1, waiting for transfers between devices, local(): lax.all_to_all(head_part, 'dy', 0, 0, axis_index_groups=groups, tiled=True)  9.21 us
    all_to_all x1, starting transfers between devices, local(): lax.all_to_all(head_part, ('dx', 'dy'), 0, 0, axis_index_groups=groups, t...  7.63 us
    ppermute x4, waiting for transfers between devices, shifted(): return lax.ppermute(value, 'dy', pairs)  6.36 us
    unnamed x24, local copies, waits for them, and re-layouts  5.42 us
  transfers between devices with their start and end apart: 7, of which 4 were waited for; matrix products, arithmetic and copies ran while one was open for 5% of the time, Pallas kernels for 12%

profile of v3, /device:TPU:24, one launch (start us, length us, event | category | flops | bytes accessed | tf_op | source)
XLA Modules:
  0.0 96.9 jit_solution(14893933550565636043)
XLA Ops:
  0.6 4.5 %collective-permute-start = (bf16[256,1152]{1,0:T(8,128)(2,1)}, bf16[256,1152]{1,0:T(8,128)(2,1)S(1)}, u32[]{:S(2)}, u32[]{:S(2)}) collective-permute-start(bf16[256,1152]{1,0:T(8,128)(2,1)} %feat_ref.1), channel_id=1, source_target_pairs={{0,1},{1,2},{2,3},{3,4},{4,5},{5,6},{6,7},{7,8},{8,9},{9,10},{10,1... | collective-permute-start | bytes 1769480 | tf_op jit(solution)/shard_map/ppermute | solution.py:25
  5.1 8.8 %collective-permute-start.1 = (bf16[256,1152]{1,0:T(8,128)(2,1)}, bf16[256,1152]{1,0:T(8,128)(2,1)S(1)}, u32[]{:S(2)}, u32[]{:S(2)}) collective-permute-start(bf16[256,1152]{1,0:T(8,128)(2,1)} %image_ref.2), channel_id=1, source_target_pairs={{0,30},{1,31},{2,0},{3,1},{4,2},{5,3},{6,4},{7,5},{8,6},{9,7},{10,... | collective-permute-start | bytes 1769480 | tf_op jit(solution)/shard_map/ppermute | solution.py:25
  15.3 0.1 pad_maximum_fusion.scale_ref
  15.4 0.0 copy-start
  15.4 1.7 %copy-done = bf16[1152,1152]{1,0:T(8,128)(2,1)S(1)} copy-done((bf16[1152,1152]{1,0:T(8,128)(2,1)S(1)}, bf16[1152,1152]{1,0:T(8,128)(2,1)}, u32[]{:S(2)}) %copy-start) | copy-done | bytes 2654232
  17.1 1.1 %copy-done.4 = bf16[256,1152]{1,0:T(8,128)(2,1)S(1)} copy-done((bf16[256,1152]{1,0:T(8,128)(2,1)S(1)}, bf16[256,1152]{1,0:T(8,128)(2,1)}, u32[]{:S(2)}) %copy-start.4) | copy-done | bytes 589848
  18.2 1.1 %copy-done.8 = bf16[256,1152]{1,0:T(8,128)(2,1)S(1)} copy-done((bf16[256,1152]{1,0:T(8,128)(2,1)S(1)}, bf16[256,1152]{1,0:T(8,128)(2,1)}, u32[]{:S(2)}) %copy-start.8) | copy-done | bytes 589848
  19.3 1.1 %copy-done.9 = s32[1152,1]{1,0:T(8,128)S(1)} copy-done((s32[1152,1]{1,0:T(8,128)S(1)}, s32[1152,1]{1,0:T(8,128)}, u32[]{:S(2)}) %copy-start.9) | copy-done | bytes 4632
  20.3 4.0 %own_blocks.1 = (bf16[1152,1280]{1,0:T(8,128)(2,1)S(1)}, bf16[256,1280]{1,0:T(8,128)(2,1)S(1)}, f32[256,1152]{1,0:T(8,128)S(1)}, f32[256,1]{1,0:T(8,128)S(1)}, b...) custom-call(f32[2]{0:T(128)S(1)} %pad_maximum_fusion.scale_ref, ...), custom_call_target="tpu_custom_call" | custom-call | flops 1736441856 | bytes 8388608 | tf_op jit(solution)/shard_map/own_blocks/pallas_call | solution.py:153
  24.4 0.0 copy-start.2
  24.4 0.0 collective-permute-done.visit_ref
  24.4 2.5 %collective-permute-done.1.image_ref = bf16[256,1152]{1,0:T(8,128)(2,1)S(1)} collective-permute-done((bf16[256,1152]{1,0:T(8,128)(2,1)}, bf16[256,1152]{1,0:T(8,128)(2,1)S(1)}, u32[]{:S(2)}, u32[]{:S(2)}) %collective-permute-start.1) | collective-permute-done | bytes 589856 | tf_op jit(solution)/shard_map/ppermute | solution.py:25
  26.9 5.3 %arrived.1 = (bf16[256,1152]{1,0:T(8,128)(2,1)}, bf16[256,1152]{1,0:T(8,128)(2,1)S(1)}, bf16[256,256]{1,0:T(8,128)(2,1)S(1)}, bf16[256,256]{1,0:T(8,128)(2,1)S(1...) custom-call(s32[1]{0:T(128)} %bitcast.core_ref, ...), custom_call_target="tpu_custom_call" | custom-call | flops 2340421632 | bytes 8388608 | tf_op jit(solution)/shard_map/arrived/pallas_call | solution.py:153
  32.2 0.0 copy-done.2
  32.2 1.2 %head_product.2 = bf16[16,328,128]{2,1,0:T(8,128)(2,1)S(1)} custom-call(bf16[576,512]{1,0:T(8,128)(2,1)S(1)} %get-tuple-element.44.back_ref, bf16[256,1280]{1,0:T(8,128)(2,1)S(1)} %get-tuple-element.42.feat_ref, bf16[256,1280]{1,0:T(8,128)(2,1)S(1)} %get-tuple-element.43.visit_ref), custom_call_target="tpu_custom_call" | custom-call | flops 754974720 | bytes 4194304 | tf_op jit(solution)/shard_map/head_product/pallas_call | solution.py:213
  33.3 0.0 copy-done.6
  33.3 1.9 %collective-permute-start.2 = (bf16[16,328,128]{2,1,0:T(8,128)(2,1)S(1)}, bf16[16,328,128]{2,1,0:T(8,128)(2,1)S(1)}, u32[]{:S(2)}, u32[]{:S(2)}) collective-permute-start(bf16[16,328,128]{2,1,0:T(8,128)(2,1)S(1)} %head_product.2), channel_id=1, source_target_pairs={{0,32},{32,0},{64,96},{96,64},{128,160},{160,128},{192,224},{224,1... | collective-permute-start | bytes 4030472 | tf_op jit(solution)/shard_map/ppermute | solution.py:340
  35.3 5.1 %collective-permute-start.3 = (bf16[256,1152]{1,0:T(8,128)(2,1)}, bf16[256,1152]{1,0:T(8,128)(2,1)}, u32[]{:S(2)}, u32[]{:S(2)}) collective-permute-start(bf16[256,1152]{1,0:T(8,128)(2,1)} %get-tuple-element.50), channel_id=1, source_target_pairs={{0,31},{1,0},{2,1},{3,2},{4,3},{5,4},{6,5},{7,6},{8,7},{9,8},{10,9... | collective-permute-start | bytes 1769480 | tf_op jit(solution)/shard_map/ppermute | solution.py:25
  40.4 0.0 collective-permute-done.2.rest_0_
  40.4 2.3 %head_product.3 = bf16[16,328,128]{2,1,0:T(8,128)(2,1)} custom-call(bf16[576,512]{1,0:T(8,128)(2,1)S(1)} %get-tuple-element.41.back_ref, bf16[256,1280]{1,0:T(8,128)(2,1)S(1)} %get-tuple-element.42.feat_ref, bf16[256,1280]{1,0:T(8,128)(2,1)S(1)} %get-tuple-element.43.visit_ref, bf16[16,328,128]{2,1,0:T(8,128)(2,1)S(1)} %collective-permute-done.2.rest_0_), custom_call_target="tpu_custom_call" | custom-call | flops 754974720 | bytes 4194304 | tf_op jit(solution)/shard_map/head_product/pallas_call | solution.py:213
  42.7 7.6 %all-to-all-start = ((bf16[16,328,128]{2,1,0:T(8,128)(2,1)}), bf16[16,328,128]{2,1,0:T(8,128)(2,1)S(1)}, u32[]{:S(2)}, u32[]{:S(2)}) async-start(bf16[16,328,128]{2,1,0:T(8,128)(2,1)} %head_product.3), calls=%async_computation | async-start | bytes 2686976 | tf_op jit(solution)/shard_map/all_to_all | solution.py:356
  50.3 0.4 fusion.2
  50.7 0.0 copy-start.3
  50.7 0.0 copy-start.7
  50.7 1.2 %fusion = bf16[256,1152]{1,0:T(8,128)(2,1)} fusion(f32[256,1152]{1,0:T(8,128)S(1)} %fusion.2, bf16[256,256]{1,0:T(8,128)(2,1)S(1)} %get-tuple-element.52, bf16[256,1152]{1,0:T(8,128)(2,1)S(1)} %get-tuple-element.33.text_low_ref), kind=kOutput, calls=%fused_computation.2 | convolution fusion | flops 151584768 | bytes 2490368 | tf_op jit(solution)/shard_map/dot_general | solution.py:42
  51.9 1.9 %collective-permute-start.4 = (bf16[256,1152]{1,0:T(8,128)(2,1)}, bf16[256,1152]{1,0:T(8,128)(2,1)}, u32[]{:S(2)}, u32[]{:S(2)}) collective-permute-start(bf16[256,1152]{1,0:T(8,128)(2,1)} %fusion), channel_id=1, source_target_pairs={{0,2},{1,3},{2,4},{3,5},{4,6},{5,7},{6,8},{7,9},{8,10},{9,11},{10,... | collective-permute-start | bytes 1769480 | tf_op jit(solution)/shard_map/ppermute | solution.py:25
  53.8 3.9 %collective-permute-done.3.home_ref = bf16[256,1152]{1,0:T(8,128)(2,1)} collective-permute-done((bf16[256,1152]{1,0:T(8,128)(2,1)}, bf16[256,1152]{1,0:T(8,128)(2,1)}, u32[]{:S(2)}, u32[]{:S(2)}) %collective-permute-start.3) | collective-permute-done | bytes 589856 | tf_op jit(solution)/shard_map/ppermute | solution.py:25
  57.7 0.0 copy-done.3
  57.7 0.0 copy-done.7
  57.7 1.5 %text_back.1 = bf16[256,1152]{1,0:T(8,128)(2,1)S(1)} custom-call(f32[256,1152]{1,0:T(8,128)S(1)} %copy-done.7, bf16[256,1152]{1,0:T(8,128)(2,1)} %collective-permute-done.3.home_ref, f32[256,1152]{1,0:T(8,128)S(1)} %copy-done.3, f32[256,1]{1,0:T(8,128)S(1)} %get-tuple-element.35.scale_col_ref), custom_call_target="tpu_custom_call" | custom-call | flops 20000000000 | bytes 4194304 | tf_op jit(solution)/shard_map/text_back/pallas_call | solution.py:283
  59.2 0.0 copy-start.10
  59.2 0.4 fusion.1
  59.6 0.4 copy-done.10
  60.0 0.4 convolution_add_fusion.1.own_ref
  60.4 0.0 copy-start.5
  60.4 10.1 %all-to-all-done.parts_ref = bf16[16,328,128]{2,1,0:T(8,128)(2,1)S(1)} async-done(((bf16[16,328,128]{2,1,0:T(8,128)(2,1)}), bf16[16,328,128]{2,1,0:T(8,128)(2,1)S(1)}, u32[]{:S(2)}, u32[]{:S(2)}) %all-to-all-start) | async-done | bytes 1343520 | tf_op jit(solution)/shard_map/all_to_all | solution.py:356
  70.5 0.9 sum_x_y.1
  71.4 10.9 %all-to-all-start.1 = ((bf16[16,24,128]{2,1,0:T(8,128)(2,1)}), bf16[16,24,128]{2,1,0:T(8,128)(2,1)S(1)}, u32[]{:S(2)}, u32[]{:S(2)}) async-start(bf16[16,24,128]{2,1,0:T(8,128)(2,1)} %sum_x_y.1), calls=%async_computation.1 | async-start | bytes 196608 | tf_op jit(solution)/shard_map/all_to_all | solution.py:369
  82.3 0.0 copy-start.1
  82.3 0.0 copy-start.11
  82.3 0.0 collective-permute-done.4.home_ref
  82.3 0.0 copy-done.5
  82.3 2.5 %grad_image.1 = f32[256,1152]{1,0:T(8,128)} custom-call(f32[256,1152]{1,0:T(8,128)S(1)} %convolution_add_fusion.1.own_ref, bf16[256,1152]{1,0:T(8,128)(2,1)} %collective-permute-done.4.home_ref, bf16[256,1152]{1,0:T(8,128)(2,1)S(1)} %copy-done.5), custom_call_target="tpu_custom_call" | custom-call | flops 2359296 | bytes 4194304 | tf_op jit(solution)/shard_map/grad_image/pallas_call | solution.py:283
  84.8 0.0 copy-done.1
  84.8 0.0 copy-done.11
  84.8 2.1 %fusion.3 = f32[256,1152]{1,0:T(8,128)} fusion(bf16[256,1152]{1,0:T(8,128)(2,1)S(1)} %copy-done.11, bf16[1152,1152]{1,0:T(8,128)(2,1)S(1)} %copy-done.1), kind=kOutput, calls=%fused_computation.6 | convolution fusion | flops 679477248 | bytes 4423680 | tf_op jit(solution)/shard_map/dot_general | solution.py:38
  86.9 9.2 %all-to-all-done.1.parts_ref = bf16[16,24,128]{2,1,0:T(8,128)(2,1)S(1)} async-done(((bf16[16,24,128]{2,1,0:T(8,128)(2,1)}), bf16[16,24,128]{2,1,0:T(8,128)(2,1)S(1)}, u32[]{:S(2)}, u32[]{:S(2)}) %all-to-all-start.1) | async-done | bytes 98336 | tf_op jit(solution)/shard_map/all_to_all | solution.py:369
  96.1 0.8 sum_z.1
  (4 shorter events, 0.0 us)
Async XLA Ops:
  0.6 23.8 %collective-permute-start = (bf16[256,1152]{1,0:T(8,128)(2,1)}, bf16[256,1152]{1,0:T(8,128)(2,1)S(1)}, u32[]{:S(2)}, u32[]{:S(2)}) collective-permute-start(bf16[256,1152]{1,0:T(8,128)(2,1)} %feat_ref.1), channel_id=1, source_target_pairs={{0,1},{1,2},{2,3},{3,4},{4,5},{5,6},{6,7},{7,8},{8,9},{9,10},{10,1... | collective-permute-start | bytes 1769480 | tf_op jit(solution)/shard_map/ppermute | solution.py:25
  5.1 21.7 %collective-permute-start.1 = (bf16[256,1152]{1,0:T(8,128)(2,1)}, bf16[256,1152]{1,0:T(8,128)(2,1)S(1)}, u32[]{:S(2)}, u32[]{:S(2)}) collective-permute-start(bf16[256,1152]{1,0:T(8,128)(2,1)} %image_ref.2), channel_id=1, source_target_pairs={{0,30},{1,31},{2,0},{3,1},{4,2},{5,3},{6,4},{7,5},{8,6},{9,7},{10,... | collective-permute-start | bytes 1769480 | tf_op jit(solution)/shard_map/ppermute | solution.py:25
  15.4 1.8 %copy-start = (bf16[1152,1152]{1,0:T(8,128)(2,1)S(1)}, bf16[1152,1152]{1,0:T(8,128)(2,1)}, u32[]{:S(2)}) copy-start(bf16[1152,1152]{1,0:T(8,128)(2,1)} %head_ref.3) | copy-start | bytes 7962628
  17.1 1.1 %copy-start.4 = (bf16[256,1152]{1,0:T(8,128)(2,1)S(1)}, bf16[256,1152]{1,0:T(8,128)(2,1)}, u32[]{:S(2)}) copy-start(bf16[256,1152]{1,0:T(8,128)(2,1)} %image_ref.2) | copy-start | bytes 1769476
  18.2 1.1 %copy-start.8 = (bf16[256,1152]{1,0:T(8,128)(2,1)S(1)}, bf16[256,1152]{1,0:T(8,128)(2,1)}, u32[]{:S(2)}) copy-start(bf16[256,1152]{1,0:T(8,128)(2,1)} %feat_ref.1) | copy-start | bytes 1769476
  19.3 1.1 %copy-start.9 = (s32[1152,1]{1,0:T(8,128)S(1)}, s32[1152,1]{1,0:T(8,128)}, u32[]{:S(2)}) copy-start(s32[1152,1]{1,0:T(8,128)} %constant.21.clone.target_ref) | copy-start | bytes 13828
  24.4 7.8 %copy-start.2 = (f32[256,1152]{1,0:T(8,128)}, f32[256,1152]{1,0:T(8,128)S(1)}, u32[]{:S(2)}) copy-start(f32[256,1152]{1,0:T(8,128)S(1)} %get-tuple-element.34.unit_ref) | copy-start | bytes 3538948
  32.2 1.2 %copy-start.6 = (f32[256,1152]{1,0:T(8,128)}, f32[256,1152]{1,0:T(8,128)S(1)}, u32[]{:S(2)}) copy-start(f32[256,1152]{1,0:T(8,128)S(1)} %get-tuple-element.48.own_ref) | copy-start | bytes 3538948
  33.3 7.1 %collective-permute-start.2 = (bf16[16,328,128]{2,1,0:T(8,128)(2,1)S(1)}, bf16[16,328,128]{2,1,0:T(8,128)(2,1)S(1)}, u32[]{:S(2)}, u32[]{:S(2)}) collective-permute-start(bf16[16,328,128]{2,1,0:T(8,128)(2,1)S(1)} %head_product.2), channel_id=1, source_target_pairs={{0,32},{32,0},{64,96},{96,64},{128,160},{160,128},{192,224},{224,1... | collective-permute-start | bytes 4030472 | tf_op jit(solution)/shard_map/ppermute | solution.py:340
  35.3 22.5 %collective-permute-start.3 = (bf16[256,1152]{1,0:T(8,128)(2,1)}, bf16[256,1152]{1,0:T(8,128)(2,1)}, u32[]{:S(2)}, u32[]{:S(2)}) collective-permute-start(bf16[256,1152]{1,0:T(8,128)(2,1)} %get-tuple-element.50), channel_id=1, source_target_pairs={{0,31},{1,0},{2,1},{3,2},{4,3},{5,4},{6,5},{7,6},{8,7},{9,8},{10,9... | collective-permute-start | bytes 1769480 | tf_op jit(solution)/shard_map/ppermute | solution.py:25
  42.7 27.8 %all-to-all-start = ((bf16[16,328,128]{2,1,0:T(8,128)(2,1)}), bf16[16,328,128]{2,1,0:T(8,128)(2,1)S(1)}, u32[]{:S(2)}, u32[]{:S(2)}) async-start(bf16[16,328,128]{2,1,0:T(8,128)(2,1)} %head_product.3), calls=%async_computation | async-start | bytes 2686976 | tf_op jit(solution)/shard_map/all_to_all | solution.py:356
  50.7 7.0 %copy-start.3 = (f32[256,1152]{1,0:T(8,128)S(1)}, f32[256,1152]{1,0:T(8,128)}, u32[]{:S(2)}) copy-start(f32[256,1152]{1,0:T(8,128)} %copy-done.2) | copy-start | bytes 3538948
  50.7 7.0 %copy-start.7 = (f32[256,1152]{1,0:T(8,128)S(1)}, f32[256,1152]{1,0:T(8,128)}, u32[]{:S(2)}) copy-start(f32[256,1152]{1,0:T(8,128)} %copy-done.6) | copy-start | bytes 3538948
  51.9 30.4 %collective-permute-start.4 = (bf16[256,1152]{1,0:T(8,128)(2,1)}, bf16[256,1152]{1,0:T(8,128)(2,1)}, u32[]{:S(2)}, u32[]{:S(2)}) collective-permute-start(bf16[256,1152]{1,0:T(8,128)(2,1)} %fusion), channel_id=1, source_target_pairs={{0,2},{1,3},{2,4},{3,5},{4,6},{5,7},{6,8},{7,9},{8,10},{9,11},{10,... | collective-permute-start | bytes 1769480 | tf_op jit(solution)/shard_map/ppermute | solution.py:25
  59.2 0.8 copy-start.10
  60.4 21.9 %copy-start.5 = (bf16[256,1152]{1,0:T(8,128)(2,1)S(1)}, bf16[256,1152]{1,0:T(8,128)(2,1)}, u32[]{:S(2)}) copy-start(bf16[256,1152]{1,0:T(8,128)(2,1)} %image_ref.2) | copy-start | bytes 1769476
  71.4 24.7 %all-to-all-start.1 = ((bf16[16,24,128]{2,1,0:T(8,128)(2,1)}), bf16[16,24,128]{2,1,0:T(8,128)(2,1)S(1)}, u32[]{:S(2)}, u32[]{:S(2)}) async-start(bf16[16,24,128]{2,1,0:T(8,128)(2,1)} %sum_x_y.1), calls=%async_computation.1 | async-start | bytes 196608 | tf_op jit(solution)/shard_map/all_to_all | solution.py:369
  82.3 2.6 %copy-start.1 = (bf16[1152,1152]{1,0:T(8,128)(2,1)S(1)}, bf16[1152,1152]{1,0:T(8,128)(2,1)}, u32[]{:S(2)}) copy-start(bf16[1152,1152]{1,0:T(8,128)(2,1)} %head_ref.3) | copy-start | bytes 7962628
  82.3 2.6 %copy-start.11 = (bf16[256,1152]{1,0:T(8,128)(2,1)S(1)}, bf16[256,1152]{1,0:T(8,128)(2,1)}, u32[]{:S(2)}) copy-start(bf16[256,1152]{1,0:T(8,128)(2,1)} %copy-done.10) | copy-start | bytes 1769476

commit v4 on v3

--- a/solution.py
+++ b/solution.py
@@ -197,7 +197,8 @@
         total = dot_nn(back_ref[:, :rows], feat_ref[:, lanes])
         total += dot_nn(back_ref[:, rows:], visit_ref[:, lanes])
         for part in range(NX * NYL):
-            peer = (yh * NYL + part % NYL) * NX + part // NYL
+            x = part // NYL
+            peer = x * NYL * NYH + (yh * NYL + part % NYL - x) % (NYL * NYH)
             cut = in_tiles(total[part * share : (part + 1) * share, :used])
             if len(rest) > 1:
                 cut += rest[0][peer].astype(jnp.float32)
@@ -343,10 +344,9 @@
     head_part = head_product(back_mine, feat_sorted, visit_sorted, head_in)
     groups = [
         [
-            ((x * NYL + yl) * NC + c) * N_DY + z * NYH + yh
-            for yh in range(NYH)
-            for yl in range(NYL)
+            ((x * NYL + y % NYL) * NC + c) * N_DY + z * NYH + y // NYL
             for x in range(NX)
+            for y in [(x + j) % (NYL * NYH) for j in range(NYL * NYH)]
         ]
         for c in range(NC)
         for z in range(NZ)

time: 98.8 us -> 98.7 us (level)
    all_to_all x1, waiting for transfers between devices: 10.1 us -> 11.7 us  [local(): lax.all_to_all(head_part, ('dx', 'dy'), 0, 0, axis_index_groups=groups, t...]
    ppermute x4, waiting for transfers between devices: 6.36 us -> 4.75 us  [shifted(): return lax.ppermute(value, 'dy', pairs)]
where the time goes in v4:
time: 98.7 us; the launch traced here: 97.1 us
  starting transfers between devices  41 us (42%)
  waiting for transfers between devices  25.6 us (26%)
  Pallas kernels  18.4 us (19%)
  local copies, waits for them, and re-layouts  5.42 us (5%)
  matrix products  4.38 us (4%)
  between operations  2.15 us (2%)
    ppermute x4, starting transfers between devices, shifted(): return lax.ppermute(value, 'dy', pairs)  20.4 us
    all_to_all x1, waiting for transfers between devices, local(): lax.all_to_all(head_part, ('dx', 'dy'), 0, 0, axis_index_groups=groups, t...  11.7 us
    all_to_all x1, starting transfers between devices, local(): lax.all_to_all(head_part, 'dy', 0, 0, axis_index_groups=groups, tiled=True)  11 us
    pallas_call x2, Pallas kernels, in_vmem(): pl.pallas_call(kernel, in_specs=[SMEM] * len(scalars) + [VMEM] * len(arra...  9.35 us
    all_to_all x1, waiting for transfers between devices, local(): lax.all_to_all(head_part, 'dy', 0, 0, axis_index_groups=groups, tiled=True)  9.2 us
    all_to_all x1, starting transfers between devices, local(): lax.all_to_all(head_part, ('dx', 'dy'), 0, 0, axis_index_groups=groups, t...  7.63 us
    unnamed x24, local copies, waits for them, and re-layouts  5.42 us
    ppermute x4, waiting for transfers between devices, shifted(): return lax.ppermute(value, 'dy', pairs)  4.75 us
  transfers between devices with their start and end apart: 7, of which 4 were waited for; matrix products, arithmetic and copies ran while one was open for 5% of the time, Pallas kernels for 12%

profile of v4, /device:TPU:24, one launch (start us, length us, event | category | flops | bytes accessed | tf_op | source)
XLA Modules:
  0.0 97.1 jit_solution(10491718201467804911)
XLA Ops:
  0.6 4.5 %collective-permute-start = (bf16[256,1152]{1,0:T(8,128)(2,1)}, bf16[256,1152]{1,0:T(8,128)(2,1)S(1)}, u32[]{:S(2)}, u32[]{:S(2)}) collective-permute-start(bf16[256,1152]{1,0:T(8,128)(2,1)} %feat_ref.1), channel_id=1, source_target_pairs={{0,1},{1,2},{2,3},{3,4},{4,5},{5,6},{6,7},{7,8},{8,9},{9,10},{10,1... | collective-permute-start | bytes 1769480 | tf_op jit(solution)/shard_map/ppermute | solution.py:25
  5.1 8.8 %collective-permute-start.1 = (bf16[256,1152]{1,0:T(8,128)(2,1)}, bf16[256,1152]{1,0:T(8,128)(2,1)S(1)}, u32[]{:S(2)}, u32[]{:S(2)}) collective-permute-start(bf16[256,1152]{1,0:T(8,128)(2,1)} %image_ref.2), channel_id=1, source_target_pairs={{0,30},{1,31},{2,0},{3,1},{4,2},{5,3},{6,4},{7,5},{8,6},{9,7},{10,... | collective-permute-start | bytes 1769480 | tf_op jit(solution)/shard_map/ppermute | solution.py:25
  15.3 0.1 pad_maximum_fusion.scale_ref
  15.4 0.0 copy-start
  15.4 1.7 %copy-done = bf16[1152,1152]{1,0:T(8,128)(2,1)S(1)} copy-done((bf16[1152,1152]{1,0:T(8,128)(2,1)S(1)}, bf16[1152,1152]{1,0:T(8,128)(2,1)}, u32[]{:S(2)}) %copy-start) | copy-done | bytes 2654232
  17.1 1.1 %copy-done.4 = bf16[256,1152]{1,0:T(8,128)(2,1)S(1)} copy-done((bf16[256,1152]{1,0:T(8,128)(2,1)S(1)}, bf16[256,1152]{1,0:T(8,128)(2,1)}, u32[]{:S(2)}) %copy-start.4) | copy-done | bytes 589848
  18.2 1.1 %copy-done.8 = bf16[256,1152]{1,0:T(8,128)(2,1)S(1)} copy-done((bf16[256,1152]{1,0:T(8,128)(2,1)S(1)}, bf16[256,1152]{1,0:T(8,128)(2,1)}, u32[]{:S(2)}) %copy-start.8) | copy-done | bytes 589848
  19.3 1.1 %copy-done.9 = s32[1152,1]{1,0:T(8,128)S(1)} copy-done((s32[1152,1]{1,0:T(8,128)S(1)}, s32[1152,1]{1,0:T(8,128)}, u32[]{:S(2)}) %copy-start.9) | copy-done | bytes 4632
  20.3 4.0 %own_blocks.1 = (bf16[1152,1280]{1,0:T(8,128)(2,1)S(1)}, bf16[256,1280]{1,0:T(8,128)(2,1)S(1)}, f32[256,1152]{1,0:T(8,128)S(1)}, f32[256,1]{1,0:T(8,128)S(1)}, b...) custom-call(f32[2]{0:T(128)S(1)} %pad_maximum_fusion.scale_ref, ...), custom_call_target="tpu_custom_call" | custom-call | flops 1736441856 | bytes 8388608 | tf_op jit(solution)/shard_map/own_blocks/pallas_call | solution.py:153
  24.4 0.0 copy-start.2
  24.4 0.0 collective-permute-done.visit_ref
  24.4 2.5 %collective-permute-done.1.image_ref = bf16[256,1152]{1,0:T(8,128)(2,1)S(1)} collective-permute-done((bf16[256,1152]{1,0:T(8,128)(2,1)}, bf16[256,1152]{1,0:T(8,128)(2,1)S(1)}, u32[]{:S(2)}, u32[]{:S(2)}) %collective-permute-start.1) | collective-permute-done | bytes 589856 | tf_op jit(solution)/shard_map/ppermute | solution.py:25
  26.9 5.3 %arrived.1 = (bf16[256,1152]{1,0:T(8,128)(2,1)}, bf16[256,1152]{1,0:T(8,128)(2,1)S(1)}, bf16[256,256]{1,0:T(8,128)(2,1)S(1)}, bf16[256,256]{1,0:T(8,128)(2,1)S(1...) custom-call(s32[1]{0:T(128)} %bitcast.core_ref, ...), custom_call_target="tpu_custom_call" | custom-call | flops 2340421632 | bytes 8388608 | tf_op jit(solution)/shard_map/arrived/pallas_call | solution.py:153
  32.2 0.0 copy-done.2
  32.2 1.2 %head_product.2 = bf16[16,328,128]{2,1,0:T(8,128)(2,1)S(1)} custom-call(bf16[576,512]{1,0:T(8,128)(2,1)S(1)} %get-tuple-element.44.back_ref, bf16[256,1280]{1,0:T(8,128)(2,1)S(1)} %get-tuple-element.42.feat_ref, bf16[256,1280]{1,0:T(8,128)(2,1)S(1)} %get-tuple-element.43.visit_ref), custom_call_target="tpu_custom_call" | custom-call | flops 754974720 | bytes 4194304 | tf_op jit(solution)/shard_map/head_product/pallas_call | solution.py:214
  33.3 0.0 copy-done.6
  33.3 1.9 %collective-permute-start.2 = (bf16[16,328,128]{2,1,0:T(8,128)(2,1)S(1)}, bf16[16,328,128]{2,1,0:T(8,128)(2,1)S(1)}, u32[]{:S(2)}, u32[]{:S(2)}) collective-permute-start(bf16[16,328,128]{2,1,0:T(8,128)(2,1)S(1)} %head_product.2), channel_id=1, source_target_pairs={{0,32},{32,0},{64,96},{96,64},{128,160},{160,128},{192,224},{224,1... | collective-permute-start | bytes 4030472 | tf_op jit(solution)/shard_map/ppermute | solution.py:341
  35.3 5.1 %collective-permute-start.3 = (bf16[256,1152]{1,0:T(8,128)(2,1)}, bf16[256,1152]{1,0:T(8,128)(2,1)}, u32[]{:S(2)}, u32[]{:S(2)}) collective-permute-start(bf16[256,1152]{1,0:T(8,128)(2,1)} %get-tuple-element.50), channel_id=1, source_target_pairs={{0,31},{1,0},{2,1},{3,2},{4,3},{5,4},{6,5},{7,6},{8,7},{9,8},{10,9... | collective-permute-start | bytes 1769480 | tf_op jit(solution)/shard_map/ppermute | solution.py:25
  40.4 0.0 collective-permute-done.2.rest_0_
  40.4 2.3 %head_product.3 = bf16[16,328,128]{2,1,0:T(8,128)(2,1)} custom-call(bf16[576,512]{1,0:T(8,128)(2,1)S(1)} %get-tuple-element.41.back_ref, bf16[256,1280]{1,0:T(8,128)(2,1)S(1)} %get-tuple-element.42.feat_ref, bf16[256,1280]{1,0:T(8,128)(2,1)S(1)} %get-tuple-element.43.visit_ref, bf16[16,328,128]{2,1,0:T(8,128)(2,1)S(1)} %collective-permute-done.2.rest_0_), custom_call_target="tpu_custom_call" | custom-call | flops 754974720 | bytes 4194304 | tf_op jit(solution)/shard_map/head_product/pallas_call | solution.py:214
  42.7 7.6 %all-to-all-start = ((bf16[16,328,128]{2,1,0:T(8,128)(2,1)}), bf16[16,328,128]{2,1,0:T(8,128)(2,1)S(1)}, u32[]{:S(2)}, u32[]{:S(2)}) async-start(bf16[16,328,128]{2,1,0:T(8,128)(2,1)} %head_product.3), calls=%async_computation | async-start | bytes 2686976 | tf_op jit(solution)/shard_map/all_to_all | solution.py:356
  50.3 0.4 fusion.2
  50.7 0.0 copy-start.3
  50.7 0.0 copy-start.7
  50.7 1.2 %fusion = bf16[256,1152]{1,0:T(8,128)(2,1)} fusion(f32[256,1152]{1,0:T(8,128)S(1)} %fusion.2, bf16[256,256]{1,0:T(8,128)(2,1)S(1)} %get-tuple-element.52, bf16[256,1152]{1,0:T(8,128)(2,1)S(1)} %get-tuple-element.33.text_low_ref), kind=kOutput, calls=%fused_computation.2 | convolution fusion | flops 151584768 | bytes 2490368 | tf_op jit(solution)/shard_map/dot_general | solution.py:42
  51.9 1.9 %collective-permute-start.4 = (bf16[256,1152]{1,0:T(8,128)(2,1)}, bf16[256,1152]{1,0:T(8,128)(2,1)}, u32[]{:S(2)}, u32[]{:S(2)}) collective-permute-start(bf16[256,1152]{1,0:T(8,128)(2,1)} %fusion), channel_id=1, source_target_pairs={{0,2},{1,3},{2,4},{3,5},{4,6},{5,7},{6,8},{7,9},{8,10},{9,11},{10,... | collective-permute-start | bytes 1769480 | tf_op jit(solution)/shard_map/ppermute | solution.py:25
  53.8 2.3 %collective-permute-done.3.home_ref = bf16[256,1152]{1,0:T(8,128)(2,1)} collective-permute-done((bf16[256,1152]{1,0:T(8,128)(2,1)}, bf16[256,1152]{1,0:T(8,128)(2,1)}, u32[]{:S(2)}, u32[]{:S(2)}) %collective-permute-start.3) | collective-permute-done | bytes 589856 | tf_op jit(solution)/shard_map/ppermute | solution.py:25
  56.1 0.0 copy-done.3
  56.1 0.0 copy-done.7
  56.1 1.5 %text_back.1 = bf16[256,1152]{1,0:T(8,128)(2,1)S(1)} custom-call(f32[256,1152]{1,0:T(8,128)S(1)} %copy-done.7, bf16[256,1152]{1,0:T(8,128)(2,1)} %collective-permute-done.3.home_ref, f32[256,1152]{1,0:T(8,128)S(1)} %copy-done.3, f32[256,1]{1,0:T(8,128)S(1)} %get-tuple-element.35.scale_col_ref), custom_call_target="tpu_custom_call" | custom-call | flops 20000000000 | bytes 4194304 | tf_op jit(solution)/shard_map/text_back/pallas_call | solution.py:284
  57.6 0.0 copy-start.10
  57.6 0.4 fusion.1
  58.0 0.4 copy-done.10
  58.4 0.4 convolution_add_fusion.1.own_ref
  58.8 0.0 copy-start.5
  58.8 11.7 %all-to-all-done.parts_ref = bf16[16,328,128]{2,1,0:T(8,128)(2,1)S(1)} async-done(((bf16[16,328,128]{2,1,0:T(8,128)(2,1)}), bf16[16,328,128]{2,1,0:T(8,128)(2,1)S(1)}, u32[]{:S(2)}, u32[]{:S(2)}) %all-to-all-start) | async-done | bytes 1343520 | tf_op jit(solution)/shard_map/all_to_all | solution.py:356
  70.5 0.9 sum_x_y.1
  71.4 11.0 %all-to-all-start.1 = ((bf16[16,24,128]{2,1,0:T(8,128)(2,1)}), bf16[16,24,128]{2,1,0:T(8,128)(2,1)S(1)}, u32[]{:S(2)}, u32[]{:S(2)}) async-start(bf16[16,24,128]{2,1,0:T(8,128)(2,1)} %sum_x_y.1), calls=%async_computation.1 | async-start | bytes 196608 | tf_op jit(solution)/shard_map/all_to_all | solution.py:369
  82.5 0.0 copy-start.1
  82.5 0.0 copy-start.11
  82.5 0.0 collective-permute-done.4.home_ref
  82.5 0.0 copy-done.5
  82.5 2.5 %grad_image.1 = f32[256,1152]{1,0:T(8,128)} custom-call(f32[256,1152]{1,0:T(8,128)S(1)} %convolution_add_fusion.1.own_ref, bf16[256,1152]{1,0:T(8,128)(2,1)} %collective-permute-done.4.home_ref, bf16[256,1152]{1,0:T(8,128)(2,1)S(1)} %copy-done.5), custom_call_target="tpu_custom_call" | custom-call | flops 2359296 | bytes 4194304 | tf_op jit(solution)/shard_map/grad_image/pallas_call | solution.py:284
  85.0 0.0 copy-done.1
  85.0 0.0 copy-done.11
  85.0 2.1 %fusion.3 = f32[256,1152]{1,0:T(8,128)} fusion(bf16[256,1152]{1,0:T(8,128)(2,1)S(1)} %copy-done.11, bf16[1152,1152]{1,0:T(8,128)(2,1)S(1)} %copy-done.1), kind=kOutput, calls=%fused_computation.6 | convolution fusion | flops 679477248 | bytes 4423680 | tf_op jit(solution)/shard_map/dot_general | solution.py:38
  87.1 9.2 %all-to-all-done.1.parts_ref = bf16[16,24,128]{2,1,0:T(8,128)(2,1)S(1)} async-done(((bf16[16,24,128]{2,1,0:T(8,128)(2,1)}), bf16[16,24,128]{2,1,0:T(8,128)(2,1)S(1)}, u32[]{:S(2)}, u32[]{:S(2)}) %all-to-all-start.1) | async-done | bytes 98336 | tf_op jit(solution)/shard_map/all_to_all | solution.py:369
  96.3 0.8 sum_z.1
  (4 shorter events, 0.0 us)
Async XLA Ops:
  0.6 23.8 %collective-permute-start = (bf16[256,1152]{1,0:T(8,128)(2,1)}, bf16[256,1152]{1,0:T(8,128)(2,1)S(1)}, u32[]{:S(2)}, u32[]{:S(2)}) collective-permute-start(bf16[256,1152]{1,0:T(8,128)(2,1)} %feat_ref.1), channel_id=1, source_target_pairs={{0,1},{1,2},{2,3},{3,4},{4,5},{5,6},{6,7},{7,8},{8,9},{9,10},{10,1... | collective-permute-start | bytes 1769480 | tf_op jit(solution)/shard_map/ppermute | solution.py:25
  5.1 21.7 %collective-permute-start.1 = (bf16[256,1152]{1,0:T(8,128)(2,1)}, bf16[256,1152]{1,0:T(8,128)(2,1)S(1)}, u32[]{:S(2)}, u32[]{:S(2)}) collective-permute-start(bf16[256,1152]{1,0:T(8,128)(2,1)} %image_ref.2), channel_id=1, source_target_pairs={{0,30},{1,31},{2,0},{3,1},{4,2},{5,3},{6,4},{7,5},{8,6},{9,7},{10,... | collective-permute-start | bytes 1769480 | tf_op jit(solution)/shard_map/ppermute | solution.py:25
  15.4 1.8 %copy-start = (bf16[1152,1152]{1,0:T(8,128)(2,1)S(1)}, bf16[1152,1152]{1,0:T(8,128)(2,1)}, u32[]{:S(2)}) copy-start(bf16[1152,1152]{1,0:T(8,128)(2,1)} %head_ref.3) | copy-start | bytes 7962628
  17.1 1.1 %copy-start.4 = (bf16[256,1152]{1,0:T(8,128)(2,1)S(1)}, bf16[256,1152]{1,0:T(8,128)(2,1)}, u32[]{:S(2)}) copy-start(bf16[256,1152]{1,0:T(8,128)(2,1)} %image_ref.2) | copy-start | bytes 1769476
  18.2 1.1 %copy-start.8 = (bf16[256,1152]{1,0:T(8,128)(2,1)S(1)}, bf16[256,1152]{1,0:T(8,128)(2,1)}, u32[]{:S(2)}) copy-start(bf16[256,1152]{1,0:T(8,128)(2,1)} %feat_ref.1) | copy-start | bytes 1769476
  19.3 1.1 %copy-start.9 = (s32[1152,1]{1,0:T(8,128)S(1)}, s32[1152,1]{1,0:T(8,128)}, u32[]{:S(2)}) copy-start(s32[1152,1]{1,0:T(8,128)} %constant.21.clone.target_ref) | copy-start | bytes 13828
  24.4 7.8 %copy-start.2 = (f32[256,1152]{1,0:T(8,128)}, f32[256,1152]{1,0:T(8,128)S(1)}, u32[]{:S(2)}) copy-start(f32[256,1152]{1,0:T(8,128)S(1)} %get-tuple-element.34.unit_ref) | copy-start | bytes 3538948
  32.2 1.2 %copy-start.6 = (f32[256,1152]{1,0:T(8,128)}, f32[256,1152]{1,0:T(8,128)S(1)}, u32[]{:S(2)}) copy-start(f32[256,1152]{1,0:T(8,128)S(1)} %get-tuple-element.48.own_ref) | copy-start | bytes 3538948
  33.3 7.1 %collective-permute-start.2 = (bf16[16,328,128]{2,1,0:T(8,128)(2,1)S(1)}, bf16[16,328,128]{2,1,0:T(8,128)(2,1)S(1)}, u32[]{:S(2)}, u32[]{:S(2)}) collective-permute-start(bf16[16,328,128]{2,1,0:T(8,128)(2,1)S(1)} %head_product.2), channel_id=1, source_target_pairs={{0,32},{32,0},{64,96},{96,64},{128,160},{160,128},{192,224},{224,1... | collective-permute-start | bytes 4030472 | tf_op jit(solution)/shard_map/ppermute | solution.py:341
  35.3 20.8 %collective-permute-start.3 = (bf16[256,1152]{1,0:T(8,128)(2,1)}, bf16[256,1152]{1,0:T(8,128)(2,1)}, u32[]{:S(2)}, u32[]{:S(2)}) collective-permute-start(bf16[256,1152]{1,0:T(8,128)(2,1)} %get-tuple-element.50), channel_id=1, source_target_pairs={{0,31},{1,0},{2,1},{3,2},{4,3},{5,4},{6,5},{7,6},{8,7},{9,8},{10,9... | collective-permute-start | bytes 1769480 | tf_op jit(solution)/shard_map/ppermute | solution.py:25
  42.7 27.8 %all-to-all-start = ((bf16[16,328,128]{2,1,0:T(8,128)(2,1)}), bf16[16,328,128]{2,1,0:T(8,128)(2,1)S(1)}, u32[]{:S(2)}, u32[]{:S(2)}) async-start(bf16[16,328,128]{2,1,0:T(8,128)(2,1)} %head_product.3), calls=%async_computation | async-start | bytes 2686976 | tf_op jit(solution)/shard_map/all_to_all | solution.py:356
  50.7 5.4 %copy-start.3 = (f32[256,1152]{1,0:T(8,128)S(1)}, f32[256,1152]{1,0:T(8,128)}, u32[]{:S(2)}) copy-start(f32[256,1152]{1,0:T(8,128)} %copy-done.2) | copy-start | bytes 3538948
  50.7 5.4 %copy-start.7 = (f32[256,1152]{1,0:T(8,128)S(1)}, f32[256,1152]{1,0:T(8,128)}, u32[]{:S(2)}) copy-start(f32[256,1152]{1,0:T(8,128)} %copy-done.6) | copy-start | bytes 3538948
  51.9 30.6 %collective-permute-start.4 = (bf16[256,1152]{1,0:T(8,128)(2,1)}, bf16[256,1152]{1,0:T(8,128)(2,1)}, u32[]{:S(2)}, u32[]{:S(2)}) collective-permute-start(bf16[256,1152]{1,0:T(8,128)(2,1)} %fusion), channel_id=1, source_target_pairs={{0,2},{1,3},{2,4},{3,5},{4,6},{5,7},{6,8},{7,9},{8,10},{9,11},{10,... | collective-permute-start | bytes 1769480 | tf_op jit(solution)/shard_map/ppermute | solution.py:25
  57.6 0.8 copy-start.10
  58.8 23.7 %copy-start.5 = (bf16[256,1152]{1,0:T(8,128)(2,1)S(1)}, bf16[256,1152]{1,0:T(8,128)(2,1)}, u32[]{:S(2)}) copy-start(bf16[256,1152]{1,0:T(8,128)(2,1)} %image_ref.2) | copy-start | bytes 1769476
  71.4 24.9 %all-to-all-start.1 = ((bf16[16,24,128]{2,1,0:T(8,128)(2,1)}), bf16[16,24,128]{2,1,0:T(8,128)(2,1)S(1)}, u32[]{:S(2)}, u32[]{:S(2)}) async-start(bf16[16,24,128]{2,1,0:T(8,128)(2,1)} %sum_x_y.1), calls=%async_computation.1 | async-start | bytes 196608 | tf_op jit(solution)/shard_map/all_to_all | solution.py:369
  82.5 2.6 %copy-start.1 = (bf16[1152,1152]{1,0:T(8,128)(2,1)S(1)}, bf16[1152,1152]{1,0:T(8,128)(2,1)}, u32[]{:S(2)}) copy-start(bf16[1152,1152]{1,0:T(8,128)(2,1)} %head_ref.3) | copy-start | bytes 7962628
  82.5 2.6 %copy-start.11 = (bf16[256,1152]{1,0:T(8,128)(2,1)S(1)}, bf16[256,1152]{1,0:T(8,128)(2,1)}, u32[]{:S(2)}) copy-start(bf16[256,1152]{1,0:T(8,128)(2,1)} %copy-done.10) | copy-start | bytes 1769476

commit v5 on v2

--- a/solution.py
+++ b/solution.py
@@ -19,17 +19,9 @@
     return (values / row_norm, row_norm)
 
 
-def shifted(value, x_steps, dy_steps):
-    if x_steps == 0:
-        pairs = [(s, (s + dy_steps) % N_DY) for s in range(N_DY)]
-        return lax.ppermute(value, "dy", pairs)
-    step = NYL * NC
-    if dy_steps == 0:
-        return lax.ppermute(value, "dx", [(s, (s + step * x_steps) % N_DX) for s in range(N_DX)])
+def shifted(value, *dy_steps):
     pairs = [
-        (p * N_DY + q, (p + step * x_steps) % N_DX * N_DY + (q + dy_steps) % N_DY)
-        for p in range(N_DX)
-        for q in range(N_DY)
+        (p * N_DY + q, p * N_DY + (q + dy_steps[p % NC]) % N_DY) for p in range(N_DX) for q in range(N_DY)
     ]
     return lax.ppermute(value, ("dx", "dy"), pairs)
 
@@ -98,8 +90,8 @@
 def arrive_kernel(
     core_ref,
     scale_ref,
-    visit_ref,
-    image_ref,
+    early_ref,
+    late_ref,
     head_ref,
     spread_ref,
     image_low_ref,
@@ -120,8 +112,11 @@
     turned_ref,
 ):
     temper, offset = scale_ref[0], scale_ref[1]
-    rows = visit_ref.shape[0]
-    image_far = unit_scaled(image_ref[...].astype(jnp.float32))[0].astype(jnp.bfloat16)
+    rows = early_ref.shape[0]
+    text_early = core_ref[0] == 0
+    visit = jnp.where(text_early, early_ref[...], late_ref[...])
+    image = jnp.where(text_early, late_ref[...], early_ref[...])
+    image_far = unit_scaled(image.astype(jnp.float32))[0].astype(jnp.bfloat16)
     image_far_ref[...] = image_far
     weight_far = weight_turned(text_low_ref[...], image_far, -1.0, temper, offset)
     weight_far_ref[...] = weight_far
@@ -129,7 +124,7 @@
     own_ref[...] = text_own
     turned_ref[:, :rows] = back_of(text_own, unit_ref[...], scale_col_ref[...]).T
 
-    next_unit, next_scale = unit_scaled(dot_nn(visit_ref[...], head_ref[...]))
+    next_unit, next_scale = unit_scaled(dot_nn(visit, head_ref[...]))
     text_next = next_unit.astype(jnp.bfloat16)
     text_next_ref[...] = text_next
     weight_on = weight_turned(text_next, image_low_ref[...], -1.0, temper, offset)
@@ -139,7 +134,7 @@
     text_part = dot_nn(weight_on, image_low_ref[...]) + dot_nn(weight_fn, image_far)
     part_ref[...] = text_part.astype(jnp.bfloat16)
     turned_ref[:, rows:] = back_of(text_part, next_unit, next_scale).T
-    sorted_ref[...] = dot_nn(visit_ref[...], spread_ref[...]).astype(jnp.bfloat16)
+    sorted_ref[...] = dot_nn(visit, spread_ref[...]).astype(jnp.bfloat16)
 
     pieces = NX * NYL
     share = turned_ref.shape[0] // (pieces * NC)
@@ -303,8 +298,9 @@
 
     low, high = jnp.bfloat16, jnp.float32
 
-    text_visit = shifted(text_feat, 0, 1)
-    image_visit = shifted(image_emb, 0, -2)
+    text_first_here = core[0] == 0
+    early = shifted(jnp.where(text_first_here, text_feat, image_emb), 1, -2)
+    late = shifted(jnp.where(text_first_here, image_emb, text_feat), -2, 1)
 
     half = -(-width // NYH // LANES) * LANES
     place = np.arange(width)
@@ -325,7 +321,7 @@
     out = in_vmem(
         arrive_kernel,
         [core, scales],
-        [text_visit, image_visit, text_head, spread, image_low, text_low, text_unit, text_scale, text_first],
+        [early, late, text_head, spread, image_low, text_low, text_unit, text_scale, text_first],
         [(block, low), (block, low), (square, low), (square, low), (square, low), (block, high)]
         + [(block, low), (sort, low)]
         + [((width // NC, 2 * rows), low)] * 2,
@@ -339,7 +335,7 @@
     head_other = head_product(back_other, feat_sorted, visit_sorted)
     head_in = lax.ppermute(head_other, "dx", [(p, p ^ 1) for p in range(N_DX)])
     text_part, _ = lax.optimization_barrier((text_part, head_other))
-    text_home = shifted(text_part, 0, -1)
+    text_home = shifted(text_part, -1, -1)
     head_part = head_product(back_mine, feat_sorted, visit_sorted, head_in)
     groups = [
         [
@@ -360,7 +356,7 @@
         text_back_kernel, [text_own, text_home, text_unit, text_scale], low, 2 * 10**10, "text_back"
     )
     image_part = dot_tn(weight_far, text_low) + dot_tn(weight_fn, text_next)
-    image_home = shifted(image_part.astype(jnp.bfloat16), 0, 2)
+    image_home = shifted(image_part.astype(jnp.bfloat16), 2, 2)
     image_own = dot_tn(weight_own, text_low) + dot_tn(weight_on, text_next)
 
     late = (image_own, text_back, image_emb, head_part)

time: 97.5 us -> 96.4 us (0.989)
  local copies, waits for them, and re-layouts: 5.42 us -> 2.24 us
  other arithmetic: 0.08 us -> 1.55 us
    ppermute x4, waiting for transfers between devices: 4.44 us -> 9.23 us  [shifted(): return lax.ppermute(value, ('dx', 'dy'), pairs)]
    all_to_all x1, waiting for transfers between devices: 12.4 us -> 8.34 us  [local(): lax.all_to_all(head_part, ('dx', 'dy'), 0, 0, axis_index_groups=groups, t...]
    unnamed x24, local copies, waits for them, and re-layouts: 5.42 us -> 2.24 us
    select_n x0 -> x1, other arithmetic: none -> 1.48 us  [local(): late = shifted(jnp.where(text_first_here, image_emb, text_feat), -2, 1)]
    all_to_all x1, starting transfers between devices: 10.5 us -> 9.28 us  [local(): lax.all_to_all(head_part, 'dy', 0, 0, axis_index_groups=groups, tiled=True)]
  transfers between devices with their start and end apart: 7 -> 7, of which waited for: 4 -> 5; matrix products, arithmetic and copies ran while one was open for 5% -> 5% of each run, Pallas kernels for 12% -> 12%
where the time goes in v5:
time: 96.4 us; the launch traced here: 95 us
  starting transfers between devices  39.5 us (41%)
  waiting for transfers between devices  26.4 us (27%)
  Pallas kernels  18.7 us (19%)
  matrix products  4.37 us (5%)
  local copies, waits for them, and re-layouts  2.24 us (2%)
  between operations  2.17 us (2%)
  other arithmetic  1.55 us (2%)
    ppermute x4, starting transfers between devices, shifted(): return lax.ppermute(value, ('dx', 'dy'), pairs)  20 us
    pallas_call x2, Pallas kernels, in_vmem(): pl.pallas_call(kernel, in_specs=[SMEM] * len(scalars) + [VMEM] * len(arra...  9.59 us
    all_to_all x1, starting transfers between devices, local(): lax.all_to_all(head_part, 'dy', 0, 0, axis_index_groups=groups, tiled=True)  9.28 us
    ppermute x4, waiting for transfers between devices, shifted(): return lax.ppermute(value, ('dx', 'dy'), pairs)  9.23 us
    all_to_all x1, waiting for transfers between devices, local(): lax.all_to_all(head_part, 'dy', 0, 0, axis_index_groups=groups, tiled=True)  8.84 us
    all_to_all x1, waiting for transfers between devices, local(): lax.all_to_all(head_part, ('dx', 'dy'), 0, 0, axis_index_groups=groups, t...  8.34 us
    all_to_all x1, starting transfers between devices, local(): lax.all_to_all(head_part, ('dx', 'dy'), 0, 0, axis_index_groups=groups, t...  7.86 us
    pallas_call x2, Pallas kernels, by_rows(): pl.pallas_call(kernel, grid=(rows // tile,), in_specs=[pl.BlockSpec((tile...  3.98 us
  transfers between devices with their start and end apart: 7, of which 5 were waited for; matrix products, arithmetic and copies ran while one was open for 5% of the time, Pallas kernels for 12%

profile of v5, /device:TPU:24, one launch (start us, length us, event | category | flops | bytes accessed | tf_op | source)
XLA Modules:
  0.0 95.0 jit_solution(5565285567678406582)
XLA Ops:
  0.6 0.0 copy-start.2
  0.7 0.0 copy-start.6
  0.7 0.0 copy-start.9
  0.7 1.5 %broadcast_select_fusion = (bf16[256,1152]{1,0:T(8,128)(2,1)S(1)}, bf16[256,1152]{1,0:T(8,128)(2,1)S(1)}) fusion(bf16[256,1152]{1,0:T(8,128)(2,1)} %image_ref.2, bf16[256,1152]{1,0:T(8,128)(2,1)} %feat_ref.1, pred[]{:T(512)S(6)} %eq.5), kind=kLoop, calls=%fused_computation.3 | loop fusion | flops 589824 | bytes 2359297 | tf_op jit(solution)/shard_map/jit(_where)/select_n | solution.py:303
  2.2 11.4 %collective-permute-start.1 = (bf16[256,1152]{1,0:T(8,128)(2,1)S(1)}, bf16[256,1152]{1,0:T(8,128)(2,1)S(1)}, u32[]{:S(2)}, u32[]{:S(2)}) collective-permute-start(bf16[256,1152]{1,0:T(8,128)(2,1)S(1)} %get-tuple-element.57), channel_id=1, source_target_pairs={{0,30},{1,31},{2,0},{3,1},{4,2},{5,3},{6,4},{7,5},{8,6},{9,7},{10,... | collective-permute-start | bytes 1769480 | tf_op jit(solution)/shard_map/ppermute | solution.py:26
  13.6 1.9 %collective-permute-start = (bf16[256,1152]{1,0:T(8,128)(2,1)S(1)}, bf16[256,1152]{1,0:T(8,128)(2,1)S(1)}, u32[]{:S(2)}, u32[]{:S(2)}) collective-permute-start(bf16[256,1152]{1,0:T(8,128)(2,1)S(1)} %get-tuple-element.58), channel_id=1, source_target_pairs={{0,1},{1,2},{2,3},{3,4},{4,5},{5,6},{6,7},{7,8},{8,9},{9,10},{10,1... | collective-permute-start | bytes 1769480 | tf_op jit(solution)/shard_map/ppermute | solution.py:26
  16.8 0.1 pad_maximum_fusion.scale_ref
  16.9 0.0 copy-done.2
  16.9 0.0 copy-done.6
  16.9 0.0 copy-done.9
  16.9 1.7 %copy-done = bf16[1152,1152]{1,0:T(8,128)(2,1)S(1)} copy-done((bf16[1152,1152]{1,0:T(8,128)(2,1)S(1)}, bf16[1152,1152]{1,0:T(8,128)(2,1)}, u32[]{:S(2)}) %copy-start) | copy-done | bytes 2654232
  18.7 4.0 %own_blocks.1 = (bf16[1152,1280]{1,0:T(8,128)(2,1)S(1)}, bf16[256,1280]{1,0:T(8,128)(2,1)S(1)}, f32[256,1152]{1,0:T(8,128)S(1)}, f32[256,1]{1,0:T(8,128)S(1)}, b...) custom-call(f32[2]{0:T(128)S(1)} %pad_maximum_fusion.scale_ref, ...), custom_call_target="tpu_custom_call" | custom-call | flops 1736441856 | bytes 8388608 | tf_op jit(solution)/shard_map/own_blocks/pallas_call | solution.py:148
  22.7 0.0 copy-start.4
  22.7 3.8 %collective-permute-done.1.late_ref = bf16[256,1152]{1,0:T(8,128)(2,1)S(1)} collective-permute-done((bf16[256,1152]{1,0:T(8,128)(2,1)S(1)}, bf16[256,1152]{1,0:T(8,128)(2,1)S(1)}, u32[]{:S(2)}, u32[]{:S(2)}) %collective-permute-start.1) | collective-permute-done | bytes 589856 | tf_op jit(solution)/shard_map/ppermute | solution.py:26
  26.5 0.3 collective-permute-done.early_ref
  26.9 5.5 %arrived.1 = (bf16[256,1152]{1,0:T(8,128)(2,1)}, bf16[256,1152]{1,0:T(8,128)(2,1)S(1)}, bf16[256,256]{1,0:T(8,128)(2,1)S(1)}, bf16[256,256]{1,0:T(8,128)(2,1)S(1...) custom-call(s32[1]{0:T(128)} %bitcast.core_ref, ...), custom_call_target="tpu_custom_call" | custom-call | flops 2340421632 | bytes 8388608 | tf_op jit(solution)/shard_map/arrived/pallas_call | solution.py:148
  32.4 0.0 copy-done.4
  32.4 1.2 %head_product.2 = bf16[16,328,128]{2,1,0:T(8,128)(2,1)S(1)} custom-call(bf16[576,512]{1,0:T(8,128)(2,1)S(1)} %get-tuple-element.44.back_ref, bf16[256,1280]{1,0:T(8,128)(2,1)S(1)} %get-tuple-element.42.feat_ref, bf16[256,1280]{1,0:T(8,128)(2,1)S(1)} %get-tuple-element.43.visit_ref), custom_call_target="tpu_custom_call" | custom-call | flops 754974720 | bytes 4194304 | tf_op jit(solution)/shard_map/head_product/pallas_call | solution.py:208
  33.6 0.0 copy-done.7
  33.6 2.4 %collective-permute-start.2 = (bf16[16,328,128]{2,1,0:T(8,128)(2,1)S(1)}, bf16[16,328,128]{2,1,0:T(8,128)(2,1)S(1)}, u32[]{:S(2)}, u32[]{:S(2)}) collective-permute-start(bf16[16,328,128]{2,1,0:T(8,128)(2,1)S(1)} %head_product.2), channel_id=1, source_target_pairs={{0,32},{32,0},{64,96},{96,64},{128,160},{160,128},{192,224},{224,1... | collective-permute-start | bytes 4030472 | tf_op jit(solution)/shard_map/ppermute | solution.py:336
  36.0 4.7 %collective-permute-start.3 = (bf16[256,1152]{1,0:T(8,128)(2,1)}, bf16[256,1152]{1,0:T(8,128)(2,1)}, u32[]{:S(2)}, u32[]{:S(2)}) collective-permute-start(bf16[256,1152]{1,0:T(8,128)(2,1)} %get-tuple-element.50), channel_id=1, source_target_pairs={{0,31},{1,0},{2,1},{3,2},{4,3},{5,4},{6,5},{7,6},{8,7},{9,8},{10,9... | collective-permute-start | bytes 1769480 | tf_op jit(solution)/shard_map/ppermute | solution.py:26
  40.7 0.0 collective-permute-done.2.rest_0_
  40.8 2.3 %head_product.3 = bf16[16,328,128]{2,1,0:T(8,128)(2,1)} custom-call(bf16[576,512]{1,0:T(8,128)(2,1)S(1)} %get-tuple-element.41.back_ref, bf16[256,1280]{1,0:T(8,128)(2,1)S(1)} %get-tuple-element.42.feat_ref, bf16[256,1280]{1,0:T(8,128)(2,1)S(1)} %get-tuple-element.43.visit_ref, bf16[16,328,128]{2,1,0:T(8,128)(2,1)S(1)} %collective-permute-done.2.rest_0_), custom_call_target="tpu_custom_call" | custom-call | flops 754974720 | bytes 4194304 | tf_op jit(solution)/shard_map/head_product/pallas_call | solution.py:208
  43.0 7.9 %all-to-all-start = ((bf16[16,328,128]{2,1,0:T(8,128)(2,1)}), bf16[16,328,128]{2,1,0:T(8,128)(2,1)S(1)}, u32[]{:S(2)}, u32[]{:S(2)}) async-start(bf16[16,328,128]{2,1,0:T(8,128)(2,1)} %head_product.3), calls=%async_computation | async-start | bytes 2686976 | tf_op jit(solution)/shard_map/all_to_all | solution.py:352
  50.9 0.4 fusion.2
  51.2 0.0 copy-start.5
  51.3 0.0 copy-start.8
  51.3 1.2 %fusion = bf16[256,1152]{1,0:T(8,128)(2,1)} fusion(f32[256,1152]{1,0:T(8,128)S(1)} %fusion.2, bf16[256,256]{1,0:T(8,128)(2,1)S(1)} %get-tuple-element.52, bf16[256,1152]{1,0:T(8,128)(2,1)S(1)} %get-tuple-element.33.text_low_ref), kind=kOutput, calls=%fused_computation.2 | convolution fusion | flops 151584768 | bytes 2490368 | tf_op jit(solution)/shard_map/dot_general | solution.py:34
  52.5 1.9 %collective-permute-start.4 = (bf16[256,1152]{1,0:T(8,128)(2,1)}, bf16[256,1152]{1,0:T(8,128)(2,1)}, u32[]{:S(2)}, u32[]{:S(2)}) collective-permute-start(bf16[256,1152]{1,0:T(8,128)(2,1)} %fusion), channel_id=1, source_target_pairs={{0,2},{1,3},{2,4},{3,5},{4,6},{5,7},{6,8},{7,9},{8,10},{9,11},{10,... | collective-permute-start | bytes 1769480 | tf_op jit(solution)/shard_map/ppermute | solution.py:26
  54.4 5.1 %collective-permute-done.3.home_ref = bf16[256,1152]{1,0:T(8,128)(2,1)} collective-permute-done((bf16[256,1152]{1,0:T(8,128)(2,1)}, bf16[256,1152]{1,0:T(8,128)(2,1)}, u32[]{:S(2)}, u32[]{:S(2)}) %collective-permute-start.3) | collective-permute-done | bytes 589856 | tf_op jit(solution)/shard_map/ppermute | solution.py:26
  59.5 0.0 copy-done.5
  59.5 1.5 %text_back.1 = bf16[256,1152]{1,0:T(8,128)(2,1)S(1)} custom-call(f32[256,1152]{1,0:T(8,128)S(1)} %copy-done.8, bf16[256,1152]{1,0:T(8,128)(2,1)} %collective-permute-done.3.home_ref, f32[256,1152]{1,0:T(8,128)S(1)} %copy-done.5, f32[256,1]{1,0:T(8,128)S(1)} %get-tuple-element.35.scale_col_ref), custom_call_target="tpu_custom_call" | custom-call | flops 20000000000 | bytes 4194304 | tf_op jit(solution)/shard_map/text_back/pallas_call | solution.py:278
  61.0 0.0 copy-start.10
  61.0 0.4 fusion.1
  61.4 0.4 copy-done.10
  61.8 0.4 convolution_add_fusion.1.own_ref
  62.2 0.0 copy-start.3
  62.2 8.3 %all-to-all-done.parts_ref = bf16[16,328,128]{2,1,0:T(8,128)(2,1)S(1)} async-done(((bf16[16,328,128]{2,1,0:T(8,128)(2,1)}), bf16[16,328,128]{2,1,0:T(8,128)(2,1)S(1)}, u32[]{:S(2)}, u32[]{:S(2)}) %all-to-all-start) | async-done | bytes 1343520 | tf_op jit(solution)/shard_map/all_to_all | solution.py:352
  70.5 0.9 sum_x_y.1
  71.4 9.3 %all-to-all-start.1 = ((bf16[16,24,128]{2,1,0:T(8,128)(2,1)}), bf16[16,24,128]{2,1,0:T(8,128)(2,1)S(1)}, u32[]{:S(2)}, u32[]{:S(2)}) async-start(bf16[16,24,128]{2,1,0:T(8,128)(2,1)} %sum_x_y.1), calls=%async_computation.1 | async-start | bytes 196608 | tf_op jit(solution)/shard_map/all_to_all | solution.py:365
  80.7 0.0 copy-start.1
  80.7 0.0 copy-start.11
  80.8 0.0 collective-permute-done.4.home_ref
  80.8 2.5 %grad_image.1 = f32[256,1152]{1,0:T(8,128)} custom-call(f32[256,1152]{1,0:T(8,128)S(1)} %convolution_add_fusion.1.own_ref, bf16[256,1152]{1,0:T(8,128)(2,1)} %collective-permute-done.4.home_ref, bf16[256,1152]{1,0:T(8,128)(2,1)S(1)} %copy-done.3), custom_call_target="tpu_custom_call" | custom-call | flops 2359296 | bytes 4194304 | tf_op jit(solution)/shard_map/grad_image/pallas_call | solution.py:278
  83.3 0.0 copy-done.11
  83.3 2.1 %fusion.3 = f32[256,1152]{1,0:T(8,128)} fusion(bf16[256,1152]{1,0:T(8,128)(2,1)S(1)} %copy-done.11, bf16[1152,1152]{1,0:T(8,128)(2,1)S(1)} %copy-done.1), kind=kOutput, calls=%fused_computation.8 | convolution fusion | flops 679477248 | bytes 4423680 | tf_op jit(solution)/shard_map/dot_general | solution.py:30
  85.4 8.8 %all-to-all-done.1.parts_ref = bf16[16,24,128]{2,1,0:T(8,128)(2,1)S(1)} async-done(((bf16[16,24,128]{2,1,0:T(8,128)(2,1)}), bf16[16,24,128]{2,1,0:T(8,128)(2,1)S(1)}, u32[]{:S(2)}, u32[]{:S(2)}) %all-to-all-start.1) | async-done | bytes 98336 | tf_op jit(solution)/shard_map/all_to_all | solution.py:365
  94.2 0.8 sum_z.1
  (5 shorter events, 0.0 us)
Async XLA Ops:
  0.6 16.3 %copy-start.2 = (bf16[256,1152]{1,0:T(8,128)(2,1)S(1)}, bf16[256,1152]{1,0:T(8,128)(2,1)}, u32[]{:S(2)}) copy-start(bf16[256,1152]{1,0:T(8,128)(2,1)} %image_ref.2) | copy-start | bytes 1769476
  0.7 16.3 %copy-start.6 = (bf16[256,1152]{1,0:T(8,128)(2,1)S(1)}, bf16[256,1152]{1,0:T(8,128)(2,1)}, u32[]{:S(2)}) copy-start(bf16[256,1152]{1,0:T(8,128)(2,1)} %feat_ref.1) | copy-start | bytes 1769476
  0.7 16.3 %copy-start.9 = (s32[1152,1]{1,0:T(8,128)S(1)}, s32[1152,1]{1,0:T(8,128)}, u32[]{:S(2)}) copy-start(s32[1152,1]{1,0:T(8,128)} %constant.22.clone.target_ref) | copy-start | bytes 13828
  2.2 24.3 %collective-permute-start.1 = (bf16[256,1152]{1,0:T(8,128)(2,1)S(1)}, bf16[256,1152]{1,0:T(8,128)(2,1)S(1)}, u32[]{:S(2)}, u32[]{:S(2)}) collective-permute-start(bf16[256,1152]{1,0:T(8,128)(2,1)S(1)} %get-tuple-element.57), channel_id=1, source_target_pairs={{0,30},{1,31},{2,0},{3,1},{4,2},{5,3},{6,4},{7,5},{8,6},{9,7},{10,... | collective-permute-start | bytes 1769480 | tf_op jit(solution)/shard_map/ppermute | solution.py:26
  13.6 13.3 %collective-permute-start = (bf16[256,1152]{1,0:T(8,128)(2,1)S(1)}, bf16[256,1152]{1,0:T(8,128)(2,1)S(1)}, u32[]{:S(2)}, u32[]{:S(2)}) collective-permute-start(bf16[256,1152]{1,0:T(8,128)(2,1)S(1)} %get-tuple-element.58), channel_id=1, source_target_pairs={{0,1},{1,2},{2,3},{3,4},{4,5},{5,6},{6,7},{7,8},{8,9},{9,10},{10,1... | collective-permute-start | bytes 1769480 | tf_op jit(solution)/shard_map/ppermute | solution.py:26
  16.9 1.8 %copy-start = (bf16[1152,1152]{1,0:T(8,128)(2,1)S(1)}, bf16[1152,1152]{1,0:T(8,128)(2,1)}, u32[]{:S(2)}) copy-start(bf16[1152,1152]{1,0:T(8,128)(2,1)} %head_ref.3) | copy-start | bytes 7962628
  22.7 9.7 %copy-start.4 = (f32[256,1152]{1,0:T(8,128)}, f32[256,1152]{1,0:T(8,128)S(1)}, u32[]{:S(2)}) copy-start(f32[256,1152]{1,0:T(8,128)S(1)} %get-tuple-element.34.unit_ref) | copy-start | bytes 3538948
  32.4 1.2 %copy-start.7 = (f32[256,1152]{1,0:T(8,128)}, f32[256,1152]{1,0:T(8,128)S(1)}, u32[]{:S(2)}) copy-start(f32[256,1152]{1,0:T(8,128)S(1)} %get-tuple-element.48.own_ref) | copy-start | bytes 3538948
  33.6 7.2 %collective-permute-start.2 = (bf16[16,328,128]{2,1,0:T(8,128)(2,1)S(1)}, bf16[16,328,128]{2,1,0:T(8,128)(2,1)S(1)}, u32[]{:S(2)}, u32[]{:S(2)}) collective-permute-start(bf16[16,328,128]{2,1,0:T(8,128)(2,1)S(1)} %head_product.2), channel_id=1, source_target_pairs={{0,32},{32,0},{64,96},{96,64},{128,160},{160,128},{192,224},{224,1... | collective-permute-start | bytes 4030472 | tf_op jit(solution)/shard_map/ppermute | solution.py:336
  36.0 23.5 %collective-permute-start.3 = (bf16[256,1152]{1,0:T(8,128)(2,1)}, bf16[256,1152]{1,0:T(8,128)(2,1)}, u32[]{:S(2)}, u32[]{:S(2)}) collective-permute-start(bf16[256,1152]{1,0:T(8,128)(2,1)} %get-tuple-element.50), channel_id=1, source_target_pairs={{0,31},{1,0},{2,1},{3,2},{4,3},{5,4},{6,5},{7,6},{8,7},{9,8},{10,9... | collective-permute-start | bytes 1769480 | tf_op jit(solution)/shard_map/ppermute | solution.py:26
  43.0 27.5 %all-to-all-start = ((bf16[16,328,128]{2,1,0:T(8,128)(2,1)}), bf16[16,328,128]{2,1,0:T(8,128)(2,1)S(1)}, u32[]{:S(2)}, u32[]{:S(2)}) async-start(bf16[16,328,128]{2,1,0:T(8,128)(2,1)} %head_product.3), calls=%async_computation | async-start | bytes 2686976 | tf_op jit(solution)/shard_map/all_to_all | solution.py:352
  51.2 8.3 %copy-start.5 = (f32[256,1152]{1,0:T(8,128)S(1)}, f32[256,1152]{1,0:T(8,128)}, u32[]{:S(2)}) copy-start(f32[256,1152]{1,0:T(8,128)} %copy-done.4) | copy-start | bytes 3538948
  51.3 8.2 %copy-start.8 = (f32[256,1152]{1,0:T(8,128)S(1)}, f32[256,1152]{1,0:T(8,128)}, u32[]{:S(2)}) copy-start(f32[256,1152]{1,0:T(8,128)} %copy-done.7) | copy-start | bytes 3538948
  52.5 28.3 %collective-permute-start.4 = (bf16[256,1152]{1,0:T(8,128)(2,1)}, bf16[256,1152]{1,0:T(8,128)(2,1)}, u32[]{:S(2)}, u32[]{:S(2)}) collective-permute-start(bf16[256,1152]{1,0:T(8,128)(2,1)} %fusion), channel_id=1, source_target_pairs={{0,2},{1,3},{2,4},{3,5},{4,6},{5,7},{6,8},{7,9},{8,10},{9,11},{10,... | collective-permute-start | bytes 1769480 | tf_op jit(solution)/shard_map/ppermute | solution.py:26
  61.0 0.8 copy-start.10
  62.2 18.6 %copy-start.3 = (bf16[256,1152]{1,0:T(8,128)(2,1)S(1)}, bf16[256,1152]{1,0:T(8,128)(2,1)}, u32[]{:S(2)}) copy-start(bf16[256,1152]{1,0:T(8,128)(2,1)} %image_ref.2) | copy-start | bytes 1769476
  71.4 22.8 %all-to-all-start.1 = ((bf16[16,24,128]{2,1,0:T(8,128)(2,1)}), bf16[16,24,128]{2,1,0:T(8,128)(2,1)S(1)}, u32[]{:S(2)}, u32[]{:S(2)}) async-start(bf16[16,24,128]{2,1,0:T(8,128)(2,1)} %sum_x_y.1), calls=%async_computation.1 | async-start | bytes 196608 | tf_op jit(solution)/shard_map/all_to_all | solution.py:365
  80.7 2.6 %copy-start.1 = (bf16[1152,1152]{1,0:T(8,128)(2,1)S(1)}, bf16[1152,1152]{1,0:T(8,128)(2,1)}, u32[]{:S(2)}) copy-start(bf16[1152,1152]{1,0:T(8,128)(2,1)} %head_ref.3) | copy-start | bytes 7962628
  80.7 2.6 %copy-start.11 = (bf16[256,1152]{1,0:T(8,128)(2,1)S(1)}, bf16[256,1152]{1,0:T(8,128)(2,1)}, u32[]{:S(2)}) copy-start(bf16[256,1152]{1,0:T(8,128)(2,1)} %copy-done.10) | copy-start | bytes 1769476
